TPU v7x, 32 devices: a whole 2x2x4 slice. The times are simulated.
32 devices in a mesh: video: 2 (over x), tm: 16 (over z, y, core).
Axes of the slice: x: 2, y: 2, z: 4, core: 2. Of those that a mesh axis runs over, the one named last changes fastest.
Arguments:
- video: bfloat16 [32, 3, 32, 960], P(('video', 'tm')), parts along dimension 0, may hold values from -6 to 6
- w_in: float32 [32, 3], replicated, may hold values from -3.5 to 3.5
- b_in: float32 [32], replicated, may hold values from -2 to 2
- w_out: float32 [3, 32], replicated, may hold values from -1 to 1
- b_out: float32 [3], replicated, may hold values from -2 to 2
- screen: float32 [3], replicated, may hold values from 0.5 to 2
Outputs:
- consistent: float32 [32, 3, 32, 960], P('video', None, 'tm'), parts along dimension 0
There are 2 independent parts, one for each index of `video`. A program takes and returns all parts, laid end to end along the dimension named above; an argument that names none is the same for every part. Nothing has to cross between parts.
All inputs are finite; a program needn't handle non-finite values.
Results may differ from a plain program's by a relative error of at most 0.0036.
Values may be sent and summed in bfloat16 or wider, within the bound.
No kernel may reach another device: no remote copies, remote signals or barrier semaphores. Data moves between devices by JAX's collectives and lax.ppermute only.
A program may use at most 64 MiB of HBM per device.

v0:
```python
import jax
import jax.numpy as jnp
from jax import lax
from jax.sharding import PartitionSpec as P

ITERS = 3


highest = lax.Precision.HIGHEST


def padded_2(cells, sides, width):
    for axis, dim in sides:
        count = lax.axis_size(axis)
        ends = count - 1
        head = lax.slice_in_dim(cells, 0, width, axis=dim)
        tail = lax.slice_in_dim(cells, cells.shape[dim] - width, cells.shape[dim], axis=dim)
        cells = jnp.concatenate(
            [
                lax.ppermute(tail, axis, [(i, (i + 1) % count) for i in range(ends)]),
                cells,
                lax.ppermute(head, axis, [((i + 1) % count, i) for i in range(ends)]),
            ],
            axis=dim,
        )
    return cells


def grade_frame(frame_in, w_in, b_in, w_out, b_out, screen):
    pixels = frame_in.astype(jnp.float32)
    before = jnp.einsum("jc,crw->jrw", w_in, pixels, precision=highest) + b_in[:, None, None]
    graded = (
        pixels
        + jnp.einsum("cj,jrw->crw", w_out, jax.nn.silu(before), precision=highest)
        + b_out[:, None, None]
    )
    padded = jnp.pad(graded, ((0, 0), (1, 1), (1, 1)))
    beside_all = (
        padded[:, 2:, 1:-1] + padded[:, :-2, 1:-1] + padded[:, 1:-1, 2:] + padded[:, 1:-1, :-2]
    )
    return ((screen[:, None, None] + 4.0) * graded - beside_all).astype(jnp.bfloat16)


def neighbours(padded):
    total = padded[2:, :, 1:-1, 1:-1] + padded[:-2, :, 1:-1, 1:-1]
    total = total + padded[1:-1, :, 2:, 1:-1] + padded[1:-1, :, :-2, 1:-1]
    total = total + padded[1:-1, :, 1:-1, 2:] + padded[1:-1, :, 1:-1, :-2]
    return total


def operate(field, screen):
    extended = padded_2(field.astype(jnp.bfloat16), (("tm", 2),), 1).astype(field.dtype)
    padded = jnp.pad(extended, ((1, 1), (0, 0), (0, 0), (1, 1)))
    return (6.0 + screen[None, :, None, None]) * field - neighbours(padded)


def channel_dot(left, right):
    return jnp.sum(left * right, axis=(0, 2, 3))


def widen(values):
    return values[None, :, None, None]


def paired_sums(residual, image):
    return lax.psum((channel_dot(residual, residual), channel_dot(residual, image)), "tm")


def shards(video, w_in, b_in, w_out, b_out, screen):
    target = lax.map(
        lambda frame_in: grade_frame(frame_in, w_in, b_in, w_out, b_out, screen), video
    )
    target = lax.all_to_all(target, "tm", split_axis=2, concat_axis=0, tiled=True)
    source = target.astype(jnp.float32)
    solution = jnp.zeros_like(source)
    residual = source
    image = operate(residual, screen)
    norm_now, product = paired_sums(residual, image)
    alpha = norm_now / product
    direction = residual
    along = image
    for sweep_index in range(ITERS):
        solution = solution + widen(alpha) * direction
        residual = residual - widen(alpha) * along
        if sweep_index + 1 < ITERS:
            image = operate(residual, screen)
            norm_next, product = paired_sums(residual, image)
            ratio = norm_next / norm_now
            alpha = norm_next / (product - ratio * norm_next / alpha)
            direction = residual + widen(ratio) * direction
            along = image + widen(ratio) * along
            norm_now = norm_next
    return solution


def solution(mesh):
    in_specs = (P(("video", "tm"), None, None, None), P(), P(), P(), P(), P())
    out_specs = P("video", None, "tm", None)
    return jax.shard_map(shards, mesh=mesh, in_specs=in_specs, out_specs=out_specs, check_vma=False)
```

profile of v0, /device:TPU:0, one launch (start us, length us, event | category | flops | bytes accessed | tf_op | source)
XLA Modules:
  0.0 145.8 jit_solution(9518942531988273726)
XLA Ops:
  0.0 0.0 copy-start
  0.0 0.0 copy-start.1
  0.0 0.0 copy-start.3
  0.0 0.0 copy-start.4
  0.0 0.0 copy-start.2
  0.0 0.7 broadcast_add_fusion
  0.7 0.0 copy-done
  0.7 2.8 %fusion.39 = f32[32,32,960]{2,0,1:T(8,128)S(1)} fusion(bf16[1,3,32,960]{3,2,1,0:T(8,128)(2,1)} %param.6, f32[32,3]{0,1:T(4,128)S(1)} %copy-done), kind=kOutput, calls=%fused_computation.61 | convolution fusion | flops 35389440 | bytes 4116864 | tf_op jit(solution)/shard_map/while/body/eval_jaxpr/jc,crw->jrw/dot_general | solution.py:31
  3.6 0.0 copy-done.1
  3.6 0.0 copy-done.3
  3.6 0.0 copy-done.4
  3.6 0.0 copy-done.2
  3.6 3.3 %fusion.15 = f32[3,32,960]{2,0,1:T(4,128)S(1)} fusion(f32[32,32,960]{2,0,1:T(8,128)S(1)} %fusion.39, f32[32]{0:T(128)S(1)} %copy-done.3, f32[3]{0:T(128)S(1)} %copy-done.4, bf16[1,3,32,960]{3,2,1,0:T(8,128)(2,1)S(1)} %copy-done.1, f32[3,32]{1,0:T(4,128)S(1)} %copy-done.2), kind=kOutput, calls=%fused_computation.11 | convolution fusion | flops 40581120 | bytes 4485644 | tf_op jit(solution)/shard_map/while/body/eval_jaxpr/cj,jrw->crw/dot_general | solution.py:34
  6.9 0.7 fusion.41
  7.6 17.3 %all_to_all.18 = bf16[1,3,32,960]{3,1,0,2:T(4,128)(2,1)S(1)} all-to-all(bf16[1,3,32,960]{3,1,0,2:T(4,128)(2,1)S(1)} %fusion.41), channel_id=1, replica_groups=mesh['video'=2,'tm'=16] {'tm'}, dimensions={2} | all-to-all | bytes 368640 | tf_op jit(solution)/shard_map/all_to_all | solution.py:73
  24.8 0.2 copy.24
  25.0 0.3 fusion.53
  25.3 1.3 collective-permute-start.1
  26.6 3.0 %collective-permute-start = (bf16[16,3,1,960]{3,2,1,0:T(2,128)(2,1)S(1)}, bf16[16,3,1,960]{3,2,1,0:T(2,128)(2,1)S(1)}, u32[]{:S(2)}, u32[]{:S(2)}) collective-permute-start(bf16[16,3,1,960]{3,2,1,0:T(2,128)(2,1)S(1)} %get-tuple-element.56), channel_id=1, source_target_pairs={{0,1},{1,2},{2,3},{3,4},{4,5},{5,6},{6,7},{7,8},{8,9},{9,10},{10,1... | collective-permute-start | bytes 276488 | tf_op jit(solution)/shard_map/ppermute | solution.py:20
  29.7 0.0 collective-permute-done.1
  29.7 1.0 collective-permute-done
  30.7 0.6 maximum_convert_fusion
  31.3 1.7 %fusion.35 = (f32[3]{0:T(128)S(1)}, f32[3]{0:T(128)S(1)}, f32[16,3,2,960]{3,2,1,0:T(2,128)S(1)}) fusion(f32[16,3,4,960]{3,2,1,0:T(4,128)S(1)} %maximum_convert_fusion, f32[3]{0:T(128)S(1)} %get-tuple-element.58, bf16[1,3,16,2,960]{4,1,3,2,0:T(4,128)(2,1)S(1)} %bitcast.33), kind=kLoop, calls=%fused_computation.48 | loop fusion | flops 1105914 | bytes 2204184 | tf_op jit(solution)/shard_map/reduce_sum | solution.py:58
  33.0 32.4 %all-reduce.6 = (f32[3]{0:T(128)S(1)}, f32[3]{0:T(128)S(1)}) all-reduce(f32[3]{0:T(128)S(1)} %get-tuple-element.32, f32[3]{0:T(128)S(1)} %get-tuple-element.23), channel_id=1, replica_groups=mesh['video'=2,'tm'=16] {'tm'}, use_global_device_ids=true, to_apply=%region_1.2 | all-reduce | flops 6 | bytes 48 | tf_op jit(solution)/shard_map/psum | solution.py:66
  65.5 0.3 fusion.49
  65.8 0.3 fusion.52
  66.1 1.3 collective-permute-start.3
  67.4 3.2 %collective-permute-start.2 = (bf16[16,3,1,960]{3,2,1,0:T(2,128)(2,1)S(1)}, bf16[16,3,1,960]{3,2,1,0:T(2,128)(2,1)S(1)}, u32[]{:S(2)}, u32[]{:S(2)}) collective-permute-start(bf16[16,3,1,960]{3,2,1,0:T(2,128)(2,1)S(1)} %get-tuple-element.54), channel_id=1, source_target_pairs={{0,1},{1,2},{2,3},{3,4},{4,5},{5,6},{6,7},{7,8},{8,9},{9,10},{10,1... | collective-permute-start | bytes 276488 | tf_op jit(solution)/shard_map/ppermute | solution.py:20
  70.6 0.0 collective-permute-done.3
  70.7 0.8 collective-permute-done.2
  71.5 0.6 maximum_convert_fusion.1
  72.1 1.7 %multiply_reduce_fusion.2 = (f32[3]{0:T(128)S(1)}, f32[3]{0:T(128)S(1)}, f32[16,3,2,960]{3,2,1,0:T(2,128)S(1)}) fusion(f32[16,3,2,960]{3,2,1,0:T(2,128)S(1)} %get-tuple-element.50, f32[3]{0:T(128)S(1)} %get-tuple-element.58, f32[16,3,4,960]{3,2,1,0:T(4,128)S(1)} %maximum_convert_fusion.1), kind=kLoop, calls=%fused_computation.58 | loop fusion | flops 1013754 | bytes 2335256 | tf_op jit(solution)/shard_map/reduce_sum | solution.py:58
  73.8 31.0 %all-reduce.5 = (f32[3]{0:T(128)S(1)}, f32[3]{0:T(128)S(1)}) all-reduce(f32[3]{0:T(128)S(1)} %get-tuple-element.22, f32[3]{0:T(128)S(1)} %get-tuple-element.21), channel_id=1, replica_groups=mesh['video'=2,'tm'=16] {'tm'}, use_global_device_ids=true, to_apply=%region_5.6 | all-reduce | flops 6 | bytes 48 | tf_op jit(solution)/shard_map/psum | solution.py:66
  104.9 0.5 fusion.46
  105.4 0.3 fusion.51
  105.6 1.3 collective-permute-start.5
  106.9 3.0 %collective-permute-start.4 = (bf16[16,3,1,960]{3,2,1,0:T(2,128)(2,1)S(1)}, bf16[16,3,1,960]{3,2,1,0:T(2,128)(2,1)S(1)}, u32[]{:S(2)}, u32[]{:S(2)}) collective-permute-start(bf16[16,3,1,960]{3,2,1,0:T(2,128)(2,1)S(1)} %get-tuple-element.52), channel_id=1, source_target_pairs={{0,1},{1,2},{2,3},{3,4},{4,5},{5,6},{6,7},{7,8},{8,9},{9,10},{10,1... | collective-permute-start | bytes 276488 | tf_op jit(solution)/shard_map/ppermute | solution.py:20
  110.0 0.0 collective-permute-done.5
  110.0 1.0 collective-permute-done.4
  111.0 0.6 maximum_convert_fusion.2
  111.7 1.7 %multiply_reduce_fusion = (f32[3]{0:T(128)S(1)}, f32[3]{0:T(128)S(1)}) fusion(f32[16,3,2,960]{3,2,1,0:T(2,128)S(1)} %get-tuple-element.44, f32[16,3,4,960]{3,2,1,0:T(4,128)S(1)} %maximum_convert_fusion.2, f32[3]{0:T(128)S(1)} %get-tuple-element.58), kind=kLoop, calls=%fused_computation.55 | loop fusion | flops 1013754 | bytes 1966616 | tf_op jit(solution)/shard_map/reduce_sum | solution.py:58
  113.4 31.0 %all-reduce.4 = (f32[3]{0:T(128)S(1)}, f32[3]{0:T(128)S(1)}) all-reduce(f32[3]{0:T(128)S(1)} %get-tuple-element.20, f32[3]{0:T(128)S(1)} %get-tuple-element.19), channel_id=1, replica_groups=mesh['video'=2,'tm'=16] {'tm'}, use_global_device_ids=true, to_apply=%region_9.10 | all-reduce | flops 6 | bytes 48 | tf_op jit(solution)/shard_map/psum | solution.py:66
  144.4 1.3 fusion.37
  (3 shorter events, 0.0 us)
Async XLA Ops:
  0.0 0.7 copy-start
  0.0 3.6 %copy-start.1 = (bf16[1,3,32,960]{3,2,1,0:T(8,128)(2,1)S(1)}, bf16[1,3,32,960]{3,2,1,0:T(8,128)(2,1)}, u32[]{:S(2)}) copy-start(bf16[1,3,32,960]{3,2,1,0:T(8,128)(2,1)} %param.6) | copy-start | bytes 552964
  0.0 3.6 %copy-start.3 = (f32[32]{0:T(128)S(1)}, f32[32]{0:T(128)}, u32[]{:S(2)}) copy-start(f32[32]{0:T(128)} %param.8) | copy-start | bytes 388
  0.0 3.6 %copy-start.4 = (f32[3]{0:T(128)S(1)}, f32[3]{0:T(128)}, u32[]{:S(2)}) copy-start(f32[3]{0:T(128)} %param.10) | copy-start | bytes 40
  0.0 3.6 %copy-start.2 = (f32[3,32]{1,0:T(4,128)S(1)}, f32[3,32]{1,0:T(4,128)}, u32[]{:S(2)}) copy-start(f32[3,32]{1,0:T(4,128)} %param.9) | copy-start | bytes 1156
  25.3 4.4 %collective-permute-start.1 = (bf16[16,3,1,960]{3,2,1,0:T(2,128)(2,1)S(1)}, bf16[16,3,1,960]{3,2,1,0:T(2,128)(2,1)S(1)}, u32[]{:S(2)}, u32[]{:S(2)}) collective-permute-start(bf16[16,3,1,960]{3,2,1,0:T(2,128)(2,1)S(1)} %get-tuple-element.57), channel_id=1, source_target_pairs={{1,0},{2,1},{3,2},{4,3},{5,4},{6,5},{7,6},{8,7},{9,8},{10,9},{11,1... | collective-permute-start | bytes 276488 | tf_op jit(solution)/shard_map/ppermute | solution.py:22
  26.6 4.1 %collective-permute-start = (bf16[16,3,1,960]{3,2,1,0:T(2,128)(2,1)S(1)}, bf16[16,3,1,960]{3,2,1,0:T(2,128)(2,1)S(1)}, u32[]{:S(2)}, u32[]{:S(2)}) collective-permute-start(bf16[16,3,1,960]{3,2,1,0:T(2,128)(2,1)S(1)} %get-tuple-element.56), channel_id=1, source_target_pairs={{0,1},{1,2},{2,3},{3,4},{4,5},{5,6},{6,7},{7,8},{8,9},{9,10},{10,1... | collective-permute-start | bytes 276488 | tf_op jit(solution)/shard_map/ppermute | solution.py:20
  66.1 4.5 %collective-permute-start.3 = (bf16[16,3,1,960]{3,2,1,0:T(2,128)(2,1)S(1)}, bf16[16,3,1,960]{3,2,1,0:T(2,128)(2,1)S(1)}, u32[]{:S(2)}, u32[]{:S(2)}) collective-permute-start(bf16[16,3,1,960]{3,2,1,0:T(2,128)(2,1)S(1)} %get-tuple-element.55), channel_id=1, source_target_pairs={{1,0},{2,1},{3,2},{4,3},{5,4},{6,5},{7,6},{8,7},{9,8},{10,9},{11,1... | collective-permute-start | bytes 276488 | tf_op jit(solution)/shard_map/ppermute | solution.py:22
  67.4 4.1 %collective-permute-start.2 = (bf16[16,3,1,960]{3,2,1,0:T(2,128)(2,1)S(1)}, bf16[16,3,1,960]{3,2,1,0:T(2,128)(2,1)S(1)}, u32[]{:S(2)}, u32[]{:S(2)}) collective-permute-start(bf16[16,3,1,960]{3,2,1,0:T(2,128)(2,1)S(1)} %get-tuple-element.54), channel_id=1, source_target_pairs={{0,1},{1,2},{2,3},{3,4},{4,5},{5,6},{6,7},{7,8},{8,9},{9,10},{10,1... | collective-permute-start | bytes 276488 | tf_op jit(solution)/shard_map/ppermute | solution.py:20
  105.6 4.4 %collective-permute-start.5 = (bf16[16,3,1,960]{3,2,1,0:T(2,128)(2,1)S(1)}, bf16[16,3,1,960]{3,2,1,0:T(2,128)(2,1)S(1)}, u32[]{:S(2)}, u32[]{:S(2)}) collective-permute-start(bf16[16,3,1,960]{3,2,1,0:T(2,128)(2,1)S(1)} %get-tuple-element.53), channel_id=1, source_target_pairs={{1,0},{2,1},{3,2},{4,3},{5,4},{6,5},{7,6},{8,7},{9,8},{10,9},{11,1... | collective-permute-start | bytes 276488 | tf_op jit(solution)/shard_map/ppermute | solution.py:22
  106.9 4.1 %collective-permute-start.4 = (bf16[16,3,1,960]{3,2,1,0:T(2,128)(2,1)S(1)}, bf16[16,3,1,960]{3,2,1,0:T(2,128)(2,1)S(1)}, u32[]{:S(2)}, u32[]{:S(2)}) collective-permute-start(bf16[16,3,1,960]{3,2,1,0:T(2,128)(2,1)S(1)} %get-tuple-element.52), channel_id=1, source_target_pairs={{0,1},{1,2},{2,3},{3,4},{4,5},{5,6},{6,7},{7,8},{8,9},{9,10},{10,1... | collective-permute-start | bytes 276488 | tf_op jit(solution)/shard_map/ppermute | solution.py:20
where the time goes:
time: 146 us
  blocking collectives  112 us (77%)
  starting transfers between devices  13.2 us (9%)
  other arithmetic  10.6 us (7%)
  matrix products  6.1 us (4%)
  waiting for transfers between devices  2.92 us (2%)
    psum x3, blocking collectives, paired_sums(): lax.psum((channel_dot(residual, residual), channel_dot(residual, image)),...  94.5 us
    all_to_all x1, blocking collectives, shards(): lax.all_to_all(target, 'tm', split_axis=2, concat_axis=0, tiled=True)  17.3 us
    ppermute x3, starting transfers between devices, padded_2(): lax.ppermute(tail, axis, [(i, (i + 1) % count) for i in range(ends)])  9.31 us
    reduce_sum x3, other arithmetic, channel_dot(): return jnp.sum(left * right, axis=(0, 2, 3))  5.1 us
    ppermute x3, starting transfers between devices, padded_2(): lax.ppermute(head, axis, [((i + 1) % count, i) for i in range(ends)])  3.88 us
    dot_general x1, matrix products, grade_frame(): jnp.einsum('cj,jrw->crw', w_out, jax.nn.silu(before), precision=highest)  3.26 us
  transfers between devices with their start and end apart: 6, of which 3 were waited for; matrix products, arithmetic and copies ran while one was open for 0% of the time, Pallas kernels for 0%

commit v1 on v0

v1 whole, which is shorter than its diff:
```python
import jax
import jax.numpy as jnp
from jax import lax
from jax.sharding import PartitionSpec as P

highest = lax.Precision.HIGHEST


def grade_frame(frame_in, w_in, b_in, w_out, b_out, screen):
    pixels = frame_in.astype(jnp.float32)
    before = jnp.einsum("jc,crw->jrw", w_in, pixels, precision=highest) + b_in[:, None, None]
    graded = (
        pixels
        + jnp.einsum("cj,jrw->crw", w_out, jax.nn.silu(before), precision=highest)
        + b_out[:, None, None]
    )
    padded = jnp.pad(graded, ((0, 0), (1, 1), (1, 1)))
    beside_all = (
        padded[:, 2:, 1:-1] + padded[:, :-2, 1:-1] + padded[:, 1:-1, 2:] + padded[:, 1:-1, :-2]
    )
    return ((screen[:, None, None] + 4.0) * graded - beside_all).astype(jnp.bfloat16)


def shifted_sum(field, dim):
    widths = [(0, 0)] * field.ndim
    widths[dim] = (1, 1)
    padded = jnp.pad(field, widths)
    size = field.shape[dim]
    return lax.slice_in_dim(padded, 0, size, axis=dim) + lax.slice_in_dim(
        padded, 2, size + 2, axis=dim
    )


def within(field):
    return shifted_sum(field, 0) + shifted_sum(field, 3)


def dot(left, right):
    return jnp.sum(left * right, axis=(0, 2, 3))


def fifth(target):
    once = shifted_sum(target, 2)
    twice = shifted_sum(once, 2)
    return dot(twice, shifted_sum(twice, 2))


def with_halo(band, axis, width):
    count = lax.axis_size(axis)
    rows = band.shape[2]
    above = lax.ppermute(
        band[:, :, rows - width :], axis, [(i, i + 1) for i in range(count - 1)]
    )
    below = lax.ppermute(band[:, :, :width], axis, [(i + 1, i) for i in range(count - 1)])
    return jnp.concatenate([above, band, below], axis=2)


def everyone(values, axis):
    count = lax.axis_size(axis)
    copies = jnp.broadcast_to(values, (count,) + values.shape)
    return jnp.sum(lax.all_to_all(copies, axis, 0, 0), axis=0)


def galerkin(nu, sigma):
    g = [sigma * nu[k] - nu[k + 1] for k in range(5)]
    l1 = g[1] / g[0]
    l2 = g[2] / g[0]
    d1 = g[2] - l1 * g[1]
    e = g[3] - l1 * g[2]
    m = e / d1
    d2 = g[4] - l2 * g[2] - m * e
    z0 = nu[0]
    z1 = nu[1] - l1 * z0
    z2 = nu[2] - l2 * z0 - m * z1
    c2 = z2 / d2
    c1 = z1 / d1 - m * c2
    c0 = z0 / g[0] - l1 * c1 - l2 * c2
    return c0, c1, c2


def widen(values):
    return values[None, :, None, None]


def shards(video, w_in, b_in, w_out, b_out, screen):
    count, me = lax.axis_size("tm"), lax.axis_index("tm")
    target = lax.map(
        lambda frame_in: grade_frame(frame_in, w_in, b_in, w_out, b_out, screen), video
    )
    rho = fifth(target.astype(jnp.float32))
    band = lax.all_to_all(target, "tm", split_axis=2, concat_axis=0, tiled=True)
    rows = band.shape[2]
    held = with_halo(band, "tm", 2).astype(jnp.float32)
    row = me * rows - 1 + jnp.arange(rows + 2)
    inside = (row >= 0) & (row < count * rows)
    once = (held[:, :, 2:] + held[:, :, :-2]) * inside[None, None, :, None]
    u0 = held[:, :, 2:-2]
    u1 = once[:, :, 1:-1]
    u2 = once[:, :, 2:] + once[:, :, :-2]
    k0 = within(u0)
    k1 = within(u1)
    y = 2.0 * k1 + within(k0)
    y1 = 2.0 * within(u2) + within(k1)
    n1 = u1 + k0
    n2 = u2 + y
    last = dot(n2, within(n2)) + dot(y, y1) + 2.0 * dot(y1, u2) + rho
    nu = jnp.stack([dot(u0, u0), dot(u0, n1), dot(n1, n1), dot(n1, n2), dot(n2, n2), last])
    nu = everyone(nu, "tm")
    c0, c1, c2 = galerkin(nu, 6.0 + screen)
    return widen(c0) * u0 + widen(c1) * n1 + widen(c2) * n2


def solution(mesh):
    in_specs = (P(("video", "tm"), None, None, None), P(), P(), P(), P(), P())
    out_specs = P("video", None, "tm", None)
    return jax.shard_map(shards, mesh=mesh, in_specs=in_specs, out_specs=out_specs, check_vma=False)
```

time: 146 us -> 56.4 us (0.39)
  blocking collectives: 112 us -> 14.7 us
  waiting for transfers between devices: 2.92 us -> 10.4 us
  other arithmetic: 10.6 us -> 13.4 us
  starting transfers between devices: 13.2 us -> 10.7 us
    psum x3 -> x0, blocking collectives: 94.5 us -> none  [paired_sums(): lax.psum((channel_dot(residual, residual), channel_dot(residual, image)),...]
    ppermute x6 -> x2, starting transfers between devices: 13.2 us -> 3.25 us  [the longest x1 1.77 us: with_halo(): lax.ppermute(band[:, :, rows - width:], axis, [(i, i + 1) for i in range(...]
    all_to_all x0 -> x1, waiting for transfers between devices: none -> 8.95 us  [shards(): band = lax.all_to_all(target, 'tm', split_axis=2, concat_axis=0, tiled=True)]
    all_to_all x0 -> x1, starting transfers between devices: none -> 7.41 us  [shards(): band = lax.all_to_all(target, 'tm', split_axis=2, concat_axis=0, tiled=True)]
    all_to_all x1, blocking collectives: 17.3 us -> 14.7 us  [everyone(): return jnp.sum(lax.all_to_all(copies, axis, 0, 0), axis=0)]
    convert_element_type x5 -> x2, other arithmetic: 2.7 us -> 0.64 us  [the longest x1 0.63 us: shards(): held = with_halo(band, 'tm', 2).astype(jnp.float32)]
    add x2 -> x7, other arithmetic: 2.04 us -> 3.96 us  [the longest x1 1.69 us: within(): return shifted_sum(field, 0) + shifted_sum(field, 3)]
    ppermute x6 -> x2, waiting for transfers between devices: 2.92 us -> 1.45 us  [the longest x1 1.45 us: with_halo(): lax.ppermute(band[:, :, :width], axis, [(i + 1, i) for i in range(count -...]
  transfers between devices with their start and end apart: 6 -> 3, of which waited for: 3 -> 2; matrix products, arithmetic and copies ran while one was open for 0% -> 3% of each run, Pallas kernels for 0% -> 0%
where the time goes in v1:
time: 56.4 us; the launch traced here: 56.1 us
  blocking collectives  14.7 us (26%)
  other arithmetic  13.4 us (24%)
  starting transfers between devices  10.7 us (19%)
  waiting for transfers between devices  10.4 us (18%)
  matrix products  6.1 us (11%)
  local copies, waits for them, and re-layouts  0.58 us (1%)
    all_to_all x1, blocking collectives, everyone(): return jnp.sum(lax.all_to_all(copies, axis, 0, 0), axis=0)  14.7 us
    all_to_all x1, waiting for transfers between devices, shards(): band = lax.all_to_all(target, 'tm', split_axis=2, concat_axis=0, tiled=True)  8.95 us
    all_to_all x1, starting transfers between devices, shards(): band = lax.all_to_all(target, 'tm', split_axis=2, concat_axis=0, tiled=True)  7.41 us
    reduce_sum x3, other arithmetic, dot(): return jnp.sum(left * right, axis=(0, 2, 3))  5.23 us
    dot_general x1, matrix products, grade_frame(): jnp.einsum('cj,jrw->crw', w_out, jax.nn.silu(before), precision=highest)  3.26 us
    dot_general x1, matrix products, grade_frame(): jnp.einsum('jc,crw->jrw', w_in, pixels, precision=highest)  2.84 us
    broadcast_in_dim x2, other arithmetic, shards(): lax.map(lambda frame_in: grade_frame(frame_in, w_in, b_in, w_out, b_out,...  2.01 us
    ppermute x1, starting transfers between devices, with_halo(): lax.ppermute(band[:, :, rows - width:], axis, [(i, i + 1) for i in range(...  1.77 us
  transfers between devices with their start and end apart: 3, of which 2 were waited for; matrix products, arithmetic and copies ran while one was open for 3% of the time, Pallas kernels for 0%

profile of v1, /device:TPU:0, one launch (start us, length us, event | category | flops | bytes accessed | tf_op | source)
XLA Modules:
  0.0 56.1 jit_solution(13345634690104963401)
XLA Ops:
  0.0 0.0 copy-start
  0.0 0.0 copy-start.1
  0.0 0.0 copy-start.5
  0.0 0.0 copy-start.4
  0.0 0.0 copy-start.3
  0.0 0.7 %broadcast_add_fusion.1 = f32[3]{0:T(128)S(1)} fusion(f32[3]{0:T(128)} %param.11), kind=kLoop, calls=%fused_computation.59 | loop fusion | flops 3 | bytes 24 | tf_op jit(solution)/shard_map/while/body/eval_jaxpr/add | solution.py:21
  0.7 0.0 copy-done
  0.7 2.8 %fusion.19 = f32[32,32,960]{2,0,1:T(8,128)S(1)} fusion(bf16[1,3,32,960]{3,2,1,0:T(8,128)(2,1)} %param.6, f32[32,3]{0,1:T(4,128)S(1)} %copy-done), kind=kOutput, calls=%fused_computation.34 | convolution fusion | flops 35389440 | bytes 4116864 | tf_op jit(solution)/shard_map/while/body/eval_jaxpr/jc,crw->jrw/dot_general | solution.py:11
  3.6 0.0 copy-done.1
  3.6 0.0 copy-done.5
  3.6 0.0 copy-done.4
  3.6 0.0 copy-done.3
  3.6 3.3 %fusion.15 = f32[3,32,960]{2,0,1:T(4,128)S(1)} fusion(f32[32,32,960]{2,0,1:T(8,128)S(1)} %fusion.19, f32[32]{0:T(128)S(1)} %copy-done.4, f32[3]{0:T(128)S(1)} %copy-done.5, bf16[1,3,32,960]{3,2,1,0:T(8,128)(2,1)S(1)} %copy-done.1, f32[3,32]{1,0:T(4,128)S(1)} %copy-done.3), kind=kOutput, calls=%fused_computation.11 | convolution fusion | flops 40581120 | bytes 4485644 | tf_op jit(solution)/shard_map/while/body/eval_jaxpr/cj,jrw->crw/dot_general | solution.py:14
  6.9 1.3 %fusion.31 = bf16[1,3,32,960]{3,1,0,2:T(4,128)(2,1)} fusion(f32[3,32,960]{2,0,1:T(4,128)S(1)} %fusion.15, f32[3]{0:T(128)S(1)} %broadcast_add_fusion.1), kind=kLoop, calls=%fused_computation.68 | loop fusion | flops 552960 | bytes 552972 | tf_op jit(solution)/shard_map/while/body/jit(dynamic_update_index_in_dim)/broadcast_in_dim | solution.py:87
  8.2 7.4 %all-to-all-start = ((bf16[1,3,32,960]{3,1,0,2:T(4,128)(2,1)}), bf16[1,3,32,960]{3,1,0,2:T(4,128)(2,1)S(1)}, u32[]{:S(2)}, u32[]{:S(2)}) async-start(bf16[1,3,32,960]{3,1,0,2:T(4,128)(2,1)} %fusion.31), calls=%async_computation | async-start | bytes 524288 | tf_op jit(solution)/shard_map/all_to_all | solution.py:91
  15.6 0.7 %fusion.30 = bf16[1,3,32,960]{3,1,2,0:T(4,128)(2,1)S(1)} fusion(f32[3,32,960]{2,0,1:T(4,128)S(1)} %fusion.15, f32[3]{0:T(128)S(1)} %broadcast_add_fusion.1), kind=kLoop, calls=%fused_computation.67 | loop fusion | flops 552960 | bytes 552972 | tf_op jit(solution)/shard_map/while/body/jit(dynamic_update_index_in_dim)/broadcast_in_dim | solution.py:87
  16.3 0.1 pad_convert_fusion
  16.5 0.1 slice_add_fusion.1
  16.6 0.1 slice_add_fusion.2
  16.7 9.0 %all-to-all-done = bf16[1,3,32,960]{3,1,0,2:T(4,128)(2,1)S(1)} async-done(((bf16[1,3,32,960]{3,1,0,2:T(4,128)(2,1)}), bf16[1,3,32,960]{3,1,0,2:T(4,128)(2,1)S(1)}, u32[]{:S(2)}, u32[]{:S(2)}) %all-to-all-start) | async-done | bytes 184352 | tf_op jit(solution)/shard_map/all_to_all | solution.py:91
  25.7 0.2 copy.27
  25.8 1.8 %collective-permute-start = (bf16[16,3,2,960]{3,2,1,0:T(2,128)(2,1)S(1)}, bf16[16,3,2,960]{3,2,1,0:T(2,128)(2,1)S(1)}, u32[]{:S(2)}, u32[]{:S(2)}) collective-permute-start(bf16[16,3,2,960]{3,2,1,0:T(2,128)(2,1)S(1)} %bitcast.34), channel_id=1, source_target_pairs={{0,1},{1,2},{2,3},{3,4},{4,5},{5,6},{6,7},{7,8},{8,9},{9,10},{10,1... | collective-permute-start | bytes 552968 | tf_op jit(solution)/shard_map/ppermute | solution.py:51
  27.6 1.5 %collective-permute-start.1 = (bf16[16,3,2,960]{3,2,1,0:T(2,128)(2,1)S(1)}, bf16[16,3,2,960]{3,2,1,0:T(2,128)(2,1)S(1)}, u32[]{:S(2)}, u32[]{:S(2)}) collective-permute-start(bf16[16,3,2,960]{3,2,1,0:T(2,128)(2,1)S(1)} %bitcast.35), channel_id=1, source_target_pairs={{1,0},{2,1},{3,2},{4,3},{5,4},{6,5},{7,6},{8,7},{9,8},{10,9},{11,1... | collective-permute-start | bytes 552968 | tf_op jit(solution)/shard_map/ppermute | solution.py:54
  29.1 0.4 multiply_reduce_fusion
  29.5 0.0 collective-permute-done
  29.5 1.5 %collective-permute-done.1 = bf16[16,3,2,960]{3,2,1,0:T(2,128)(2,1)S(1)} collective-permute-done((bf16[16,3,2,960]{3,2,1,0:T(2,128)(2,1)S(1)}, bf16[16,3,2,960]{3,2,1,0:T(2,128)(2,1)S(1)}, u32[]{:S(2)}, u32[]{:S(2)}) %collective-permute-start.1) | collective-permute-done | bytes 184352 | tf_op jit(solution)/shard_map/ppermute | solution.py:54
  30.9 0.6 %maximum_convert_fusion = f32[16,3,6,960]{3,2,1,0:T(8,128)S(1)} fusion(bf16[16,3,2,960]{3,2,1,0:T(2,128)(2,1)S(1)} %collective-permute-done.1, bf16[16,3,2,960]{3,2,1,0:T(2,128)(2,1)S(1)} %bitcast.36, bf16[16,3,2,960]{3,2,1,0:T(2,128)(2,1)S(1)} %collective-permute-done), kind=kLoop, calls=%fused_computation.14 | loop fusion | flops 1658880 | bytes 1658880 | tf_op jit(solution)/shard_map/convert_element_type | solution.py:93
  31.6 0.3 fusion.18
  31.9 0.4 fusion.29
  32.3 0.0 copy-start.2
  32.3 0.7 %fusion.28 = (f32[16,3,2,960]{3,2,1,0:T(2,128)S(1)}, bf16[16,3,2,960]{3,2,1,0:T(2,128)(2,1)S(1)}) fusion(bf16[16,3,2,960]{3,2,1,0:T(2,128)(2,1)S(1)} %collective-permute-done.1, bf16[16,3,2,960]{3,2,1,0:T(2,128)(2,1)S(1)} %bitcast.37, bf16[16,3,2,960]{3,2,1,0:T(2,128)(2,1)S(1)} %collective-permute-done), kind=kLoop, calls=%fused_computation.65 | loop fusion | flops 645120 | bytes 1105920 | tf_op jit(solution)/shard_map/slice | solution.py:97
  33.0 1.7 %add_add_fusion.2 = (f32[16,3,2,960]{3,2,1,0:T(2,128)S(1)}, f32[16,3,2,960]{3,2,1,0:T(2,128)S(1)}) fusion(f32[16,3,2,960]{3,2,1,0:T(2,128)S(1)} %get-tuple-element.50, f32[16,3,2,960]{3,2,1,0:T(2,128)S(1)} %get-tuple-element.48), kind=kLoop, calls=%fused_computation.28 | loop fusion | flops 552960 | bytes 1474560 | tf_op jit(solution)/shard_map/add | solution.py:35
  34.7 3.3 %multiply_reduce_fusion.2 = (f32[3]{0:T(128)S(1)}, f32[3]{0:T(128)S(1)}, f32[16,3,2,960]{3,2,1,0:T(2,128)S(1)}) fusion(f32[16,3,2,960]{3,2,1,0:T(2,128)S(1)} %get-tuple-element.51, f32[16,3,2,960]{3,2,1,0:T(2,128)S(1)} %get-tuple-element.53, f32[16,3,2,960]{3,2,1,0:T(2,128)S(1)} %get-tuple-element.52), kind=kLoop, calls=%fused_computation.22 | loop fusion | flops 1566714 | bytes 1474584 | tf_op jit(solution)/shard_map/reduce_sum | solution.py:39
  37.9 0.2 add.245
  38.1 1.6 %multiply_reduce_fusion.3 = (f32[3]{0:T(128)S(1)}, f32[3]{0:T(128)S(1)}, f32[3]{0:T(128)S(1)}, f32[3]{0:T(128)S(1)}, f32[3]{0:T(128)S(1)}, /*index=5*/f32[3]{0:T(128)S(1)}, f32[16,3,2,960]{3,2,1,0:T(2,128)S(1)}) fusion(f32[16,3,2,960]{3,2,1,0:T(2,128)S(1)} %add.245, bf16[16,3,2,960]{3,2,1,0:T(2,128)(2,1)S(1)} %get-tuple-element.49, ...), kind=kLoop, calls=%fused_computation.24 | loop fusion | flops 1566702 | bytes 1658952 | tf_op jit(solution)/shard_map/reduce_sum | solution.py:39
  39.8 0.1 copy.20
  39.9 14.7 %all_to_all.23 = f32[16,6,3]{1,2,0:T(4,128)S(1)} all-to-all(f32[16,6,3]{1,2,0:T(4,128)S(1)} %broadcast_in_dim.20), channel_id=1, replica_groups=mesh['video'=2,'tm'=16] {'tm'}, dimensions={0} | all-to-all | bytes 2304 | tf_op jit(solution)/shard_map/all_to_all | solution.py:61
  54.6 0.3 slice_reduce_fusion.2
  54.9 0.0 copy-done.2
  54.9 1.1 %multiply_add_fusion = f32[16,3,2,960]{3,2,1,0:T(2,128)} fusion(f32[16,3,2,960]{3,2,1,0:T(2,128)S(1)} %add.245, f32[16,3,2,960]{3,2,1,0:T(2,128)S(1)} %get-tuple-element.47, bf16[16,3,2,960]{3,2,1,0:T(2,128)(2,1)S(1)} %get-tuple-element.49, f32[3]{0:T(128)S(1)} %get-tuple-element.45, f32[3]{0:T(128)S(1)} %get-tuple-element.44, f32[3]{0:T(128)S(1)} %get-tuple-element.43), kind=kLoop, calls=%fused_computation.20 | loop fusion | flops 552960 | bytes 1290276 | tf_op jit(solution)/shard_map/add | solution.py:110
  (6 shorter events, 0.1 us)
Async XLA Ops:
  0.0 0.7 %copy-start = (f32[32,3]{0,1:T(4,128)S(1)}, f32[32,3]{0,1:T(4,128)}, u32[]{:S(2)}) copy-start(f32[32,3]{0,1:T(4,128)} %param.7) | copy-start | bytes 1156
  0.0 3.6 %copy-start.1 = (bf16[1,3,32,960]{3,2,1,0:T(8,128)(2,1)S(1)}, bf16[1,3,32,960]{3,2,1,0:T(8,128)(2,1)}, u32[]{:S(2)}) copy-start(bf16[1,3,32,960]{3,2,1,0:T(8,128)(2,1)} %param.6) | copy-start | bytes 552964
  0.0 3.6 %copy-start.5 = (f32[3]{0:T(128)S(1)}, f32[3]{0:T(128)}, u32[]{:S(2)}) copy-start(f32[3]{0:T(128)} %param.10) | copy-start | bytes 40
  0.0 3.6 %copy-start.4 = (f32[32]{0:T(128)S(1)}, f32[32]{0:T(128)}, u32[]{:S(2)}) copy-start(f32[32]{0:T(128)} %param.8) | copy-start | bytes 388
  0.0 3.6 %copy-start.3 = (f32[3,32]{1,0:T(4,128)S(1)}, f32[3,32]{1,0:T(4,128)}, u32[]{:S(2)}) copy-start(f32[3,32]{1,0:T(4,128)} %param.9) | copy-start | bytes 1156
  8.2 17.5 %all-to-all-start = ((bf16[1,3,32,960]{3,1,0,2:T(4,128)(2,1)}), bf16[1,3,32,960]{3,1,0,2:T(4,128)(2,1)S(1)}, u32[]{:S(2)}, u32[]{:S(2)}) async-start(bf16[1,3,32,960]{3,1,0,2:T(4,128)(2,1)} %fusion.31), calls=%async_computation | async-start | bytes 524288 | tf_op jit(solution)/shard_map/all_to_all | solution.py:91
  25.8 3.7 %collective-permute-start = (bf16[16,3,2,960]{3,2,1,0:T(2,128)(2,1)S(1)}, bf16[16,3,2,960]{3,2,1,0:T(2,128)(2,1)S(1)}, u32[]{:S(2)}, u32[]{:S(2)}) collective-permute-start(bf16[16,3,2,960]{3,2,1,0:T(2,128)(2,1)S(1)} %bitcast.34), channel_id=1, source_target_pairs={{0,1},{1,2},{2,3},{3,4},{4,5},{5,6},{6,7},{7,8},{8,9},{9,10},{10,1... | collective-permute-start | bytes 552968 | tf_op jit(solution)/shard_map/ppermute | solution.py:51
  27.6 3.3 %collective-permute-start.1 = (bf16[16,3,2,960]{3,2,1,0:T(2,128)(2,1)S(1)}, bf16[16,3,2,960]{3,2,1,0:T(2,128)(2,1)S(1)}, u32[]{:S(2)}, u32[]{:S(2)}) collective-permute-start(bf16[16,3,2,960]{3,2,1,0:T(2,128)(2,1)S(1)} %bitcast.35), channel_id=1, source_target_pairs={{1,0},{2,1},{3,2},{4,3},{5,4},{6,5},{7,6},{8,7},{9,8},{10,9},{11,1... | collective-permute-start | bytes 552968 | tf_op jit(solution)/shard_map/ppermute | solution.py:54
  32.3 22.6 %copy-start.2 = (f32[3]{0:T(128)S(1)}, f32[3]{0:T(128)}, u32[]{:S(2)}) copy-start(f32[3]{0:T(128)} %param.11) | copy-start | bytes 40

commit v2 on v1

v2 whole, which is shorter than its diff:
```python
import functools

import jax
import jax.numpy as jnp
from jax import lax
from jax.experimental import pallas as pl
from jax.experimental.pallas import tpu as pltpu
from jax.sharding import PartitionSpec as P

BLOCKS = 8
LANES = 128
AXIS = "tm"


def lanes_of(shape):
    return lax.broadcasted_iota(jnp.int32, shape, len(shape) - 1)


def grade_kernel(w_in, b_in, w_out, b_out, screen, video, chunks, rho, padded, graded, blocks):
    channels, rows, columns = video.shape[1:]
    units = w_in.shape[0]
    across = padded.shape[2]
    width = columns // BLOCKS
    halo = (LANES - width) // 2
    dests = chunks.shape[0]

    for c in range(channels):
        padded[c, :, :] = jnp.zeros((rows, across), jnp.float32)
        padded[c, :, :columns] = video[0, c].astype(jnp.float32)

    def grade(step, _):
        at = pl.ds(pl.multiple_of(step * LANES, LANES), LANES)
        pixels = [padded[c, :, at] for c in range(channels)]
        total = [pixels[c] + b_out[c] for c in range(channels)]
        for j in range(units):
            half = pixels[0] * (0.5 * w_in[j, 0])
            for c in range(1, channels):
                half = half + pixels[c] * (0.5 * w_in[j, c])
            half = half + 0.5 * b_in[j]
            unit = half + half * jnp.tanh(half)
            for c in range(channels):
                total[c] = total[c] + w_out[c, j] * unit
        inside = step * LANES + lanes_of((rows, LANES)) < columns
        for c in range(channels):
            graded[c, :, at] = jnp.where(inside, total[c], 0.0)
        return 0

    lax.fori_loop(0, across // LANES, grade, 0)

    row = lax.broadcasted_iota(jnp.int32, (rows, across), 0)
    lane = lanes_of((8, LANES))
    for c in range(channels):
        g = graded[c]
        above = jnp.where(row == 0, 0.0, pltpu.roll(g, 1, 0))
        below = jnp.where(row == rows - 1, 0.0, pltpu.roll(g, rows - 1, 0))
        beside = pltpu.roll(g, 1, 1) + pltpu.roll(g, across - 1, 1)
        target = (screen[c] + 4.0) * g - (above + below + beside)
        inside = lanes_of((rows, across)) < columns
        target = jnp.where(inside, target, 0.0).astype(jnp.bfloat16).astype(jnp.float32)
        for first in range(0, rows, 8):
            tile = target[first : first + 8]
            parts = []
            for s in range(BLOCKS):
                start = s * width - halo
                v, off = start // LANES, start % LANES
                low = jnp.zeros((8, LANES), jnp.float32)
                if v >= 0:
                    low = pltpu.roll(tile[:, v * LANES : (v + 1) * LANES], (LANES - off) % LANES, 1)
                high = pltpu.roll(tile[:, (v + 1) * LANES : (v + 2) * LANES], LANES - off, 1)
                parts.append(jnp.where(lane < LANES - off, low, high))
            blocks[c, first : first + 8] = jnp.swapaxes(jnp.stack(parts, axis=0), 0, 1)

    for c in range(channels):
        field = [blocks[c, r] for r in range(rows)]
        for _ in range(2):
            field = [
                sum(field[i] for i in (r - 1, r + 1) if 0 <= i < rows) for r in range(rows)
            ]
        total = field[0] * field[1]
        for r in range(1, rows - 1):
            total = total + field[r] * field[r + 1]
        rho[c] = total + total
        zero = jnp.zeros((BLOCKS, LANES), jnp.float32)

        def line(r):
            return blocks[c, r] if 0 <= r < rows else zero

        for d in range(dests):
            if d % 2 == 0:
                order = [2 * d - 2, 2 * d - 1, 2 * d, 2 * d + 1]
            else:
                order = [2 * d + 3, 2 * d + 2, 2 * d + 1, 2 * d]
            for p in range(2):
                pair = jnp.concatenate([line(order[2 * p]), line(order[2 * p + 1])], axis=0)
                chunks[d, p, c] = pair.astype(jnp.bfloat16)


def within(field, mask):
    zero = jnp.zeros_like(field[:1])
    frames = jnp.concatenate([field[1:], zero], axis=0) + jnp.concatenate([zero, field[:-1]], axis=0)
    beside = pltpu.roll(field, 1, 2) + pltpu.roll(field, LANES - 1, 2)
    return frames + jnp.where(mask, beside, 0.0)


def moment_kernel(columns, edge, held, sibling, rho, sums, first, second):
    frames, _, channels = held.shape[:3]
    width = columns // BLOCKS
    halo = (LANES - width) // 2
    shape = (frames, 2 * BLOCKS, LANES)
    lane = lanes_of(shape)
    column = (lax.broadcasted_iota(jnp.int32, shape, 1) % BLOCKS) * width - halo + lane
    mask = (column >= 0) & (column < columns)
    own = lanes_of((2 * BLOCKS, LANES))
    own = (own >= halo) & (own < halo + width)
    inside = edge[0]
    out_lane = lanes_of((1, LANES))
    result = jnp.zeros((1, LANES), jnp.float32)
    for c in range(channels):
        far = held[:, 0, c].astype(jnp.float32)
        u0 = held[:, 1, c].astype(jnp.float32)
        near = sibling[:, c].astype(jnp.float32)
        b0, b1 = far[:, :BLOCKS], far[:, BLOCKS:]
        b2, b3 = u0[:, :BLOCKS], u0[:, BLOCKS:]
        b5, b4 = near[:, :BLOCKS], near[:, BLOCKS:]
        u1 = jnp.concatenate([b1 + b3, b2 + b4], axis=1)
        u2 = jnp.concatenate([b0 + (1.0 + inside) * b2 + b4, b1 + 2.0 * b3 + b5], axis=1)
        k0 = within(u0, mask)
        k1 = within(u1, mask)
        y = 2.0 * k1 + within(k0, mask)
        y1 = 2.0 * within(u2, mask) + within(k1, mask)
        n1 = u1 + k0
        n2 = u2 + y
        first[c] = n1
        second[c] = n2
        moments = [
            u0 * u0,
            u0 * n1,
            n1 * n1,
            n1 * n2,
            n2 * n2,
            n2 * within(n2, mask) + y * y1 + 2.0 * (y1 * u2),
        ]
        for k, product in enumerate(moments):
            total = jnp.sum(product, axis=0)
            total = total[:BLOCKS] + total[BLOCKS:]
            if k == len(moments) - 1:
                total = total + rho[c]
            total = jnp.where(own[:BLOCKS], total, 0.0)
            total = jnp.sum(total, axis=0, keepdims=True)
            total = jnp.sum(total, axis=1, keepdims=True)
            result = jnp.where(out_lane == BLOCKS * k + c, total, result)
    sums[...] = jnp.broadcast_to(result[None], sums.shape)


def combine_kernel(columns, screen, sums, held, first, second, out):
    frames, _, channels = held.shape[:3]
    width = columns // BLOCKS
    halo = (LANES - width) // 2
    lane = lanes_of((1, LANES))
    total = jnp.sum(sums[...], axis=0)
    nu = [total] + [pltpu.roll(total, LANES - BLOCKS * k, 1) for k in range(1, 6)]
    sigma = jnp.full((1, LANES), 1.0, jnp.float32)
    for c in range(channels):
        sigma = jnp.where(lane == c, 6.0 + screen[c], sigma)
    g = [sigma * nu[k] - nu[k + 1] for k in range(5)]
    l1 = g[1] / g[0]
    l2 = g[2] / g[0]
    d1 = g[2] - l1 * g[1]
    e = g[3] - l1 * g[2]
    m = e / d1
    d2 = g[4] - l2 * g[2] - m * e
    z0 = nu[0]
    z1 = nu[1] - l1 * z0
    z2 = nu[2] - l2 * z0 - m * z1
    c2 = z2 / d2
    c1 = z1 / d1 - m * c2
    c0 = z0 / g[0] - l1 * c1 - l2 * c2

    tile_lane = lanes_of((8, LANES))
    tiles = -(-columns // LANES)
    for c in range(channels):
        w0, w1, w2 = (
            jnp.sum(jnp.where(lane == c, w, 0.0), axis=1, keepdims=True)[None] for w in (c0, c1, c2)
        )
        for row in range(2):
            part = slice(row * BLOCKS, (row + 1) * BLOCKS)
            x = (
                w0 * held[:, 1, c, part].astype(jnp.float32)
                + w1 * first[c, :, part]
                + w2 * second[c, :, part]
            )
            for f in range(0, frames, 8):
                turned = jnp.swapaxes(x[f : f + 8], 0, 1)
                moved = [
                    pltpu.roll(turned[s], (s * width - halo) % LANES, 1) for s in range(BLOCKS)
                ]
                for t in range(tiles):
                    bound = width * (t + 1) - LANES * t
                    piece = moved[t]
                    if t + 1 < BLOCKS:
                        piece = jnp.where(tile_lane < bound, moved[t], moved[t + 1])
                    count = min(LANES, columns - LANES * t)
                    out[c, row, f : f + 8, LANES * t : LANES * t + count] = piece[:, :count]


def smem():
    return pl.BlockSpec(memory_space=pltpu.SMEM)


def vmem():
    return pl.BlockSpec(memory_space=pltpu.VMEM)


def shards(video, w_in, b_in, w_out, b_out, screen):
    count, me = lax.axis_size(AXIS), lax.axis_index(AXIS)
    _, channels, rows, columns = video.shape
    frames = count
    across = -(-columns // LANES) * LANES
    chunks, rho = pl.pallas_call(
        grade_kernel,
        out_shape=(
            jax.ShapeDtypeStruct((count, 2, channels, 2 * BLOCKS, LANES), jnp.bfloat16),
            jax.ShapeDtypeStruct((channels, BLOCKS, LANES), jnp.float32),
        ),
        in_specs=[smem()] * 5 + [vmem()],
        out_specs=(vmem(), vmem()),
        scratch_shapes=[
            pltpu.VMEM((channels, rows, across), jnp.float32),
            pltpu.VMEM((channels, rows, across), jnp.float32),
            pltpu.VMEM((channels, rows, BLOCKS, LANES), jnp.float32),
        ],
        name="grade",
    )(w_in, b_in, w_out, b_out, screen, video)
    held = lax.all_to_all(chunks, AXIS, 0, 0)
    sibling = lax.ppermute(held[:, 1], AXIS, [(i, i ^ 1) for i in range(count)])
    edge = jnp.where((me == 0) | (me == count - 1), 0.0, 1.0).reshape(1)
    field = jax.ShapeDtypeStruct((channels, frames, 2 * BLOCKS, LANES), jnp.float32)
    sums, first, second = pl.pallas_call(
        functools.partial(moment_kernel, columns),
        out_shape=(jax.ShapeDtypeStruct((count, 1, LANES), jnp.float32), field, field),
        in_specs=[smem()] + [vmem()] * 3,
        out_specs=(vmem(),) * 3,
        name="moments",
    )(edge, held, sibling, rho)
    sums = lax.all_to_all(sums, AXIS, 0, 0)
    out = pl.pallas_call(
        functools.partial(combine_kernel, columns),
        out_shape=jax.ShapeDtypeStruct((channels, 2, frames, columns), jnp.float32),
        in_specs=[smem()] + [vmem()] * 4,
        out_specs=vmem(),
        name="combine",
    )(screen, sums, held, first, second)
    out = jnp.where(me % 2 == 0, out, out[:, ::-1])
    return out.transpose(2, 0, 1, 3)


def solution(mesh):
    in_specs = (P(("video", AXIS), None, None, None), P(), P(), P(), P(), P())
    out_specs = P("video", None, AXIS, None)
    return jax.shard_map(shards, mesh=mesh, in_specs=in_specs, out_specs=out_specs, check_vma=False)
```

time: 56.4 us -> 46.7 us (0.83)
  other arithmetic: 13.4 us -> 1.16 us
  Pallas kernels: 0 us -> 10.4 us
  starting transfers between devices: 10.7 us -> 3.7 us
  matrix products: 6.1 us -> 0 us
  blocking collectives: 14.7 us -> 19.6 us
  local copies, waits for them, and re-layouts: 0.58 us -> 3.69 us
  waiting for transfers between devices: 10.4 us -> 7.72 us
    pallas_call x0 -> x3, Pallas kernels: none -> 10.4 us  [the longest x1 4.81 us: shards(): pl.pallas_call(grade_kernel, out_shape=(jax.ShapeDtypeStruct((count, 2, c...]
    dot_general x2 -> x0, matrix products: 6.1 us -> none  [the longest x1 3.26 us: grade_frame(): jnp.einsum('cj,jrw->crw', w_out, jax.nn.silu(before), precision=highest)]
    reduce_sum x4 -> x0, other arithmetic: 5.26 us -> none  [the longest x3 5.23 us: dot(): return jnp.sum(left * right, axis=(0, 2, 3))]
    all_to_all x1, blocking collectives: 14.7 us -> 19.6 us  [shards(): held = lax.all_to_all(chunks, AXIS, 0, 0)]
    add x7 -> x0, other arithmetic: 3.96 us -> none  [the longest x1 1.69 us: within(): return shifted_sum(field, 0) + shifted_sum(field, 3)]
    all_to_all x1, starting transfers between devices: 7.41 us -> 3.52 us  [shards(): sums = lax.all_to_all(sums, AXIS, 0, 0)]
    ppermute x2 -> x1, starting transfers between devices: 3.25 us -> 0.18 us  [shards(): sibling = lax.ppermute(held[:, 1], AXIS, [(i, i ^ 1) for i in range(count)])]
    unnamed x12 -> x7, local copies, waits for them, and re-layouts: 0.03 us -> 2.63 us
  transfers between devices with their start and end apart: 3 -> 2, of which waited for: 2 -> 2; matrix products, arithmetic and copies ran while one was open for 3% -> 0% of each run, Pallas kernels for 0% -> 0%
where the time goes in v2:
time: 46.7 us; the launch traced here: 46.3 us
  blocking collectives  19.6 us (42%)
  Pallas kernels  10.4 us (22%)
  waiting for transfers between devices  7.72 us (17%)
  starting transfers between devices  3.7 us (8%)
  local copies, waits for them, and re-layouts  3.69 us (8%)
  other arithmetic  1.16 us (2%)
    all_to_all x1, blocking collectives, shards(): held = lax.all_to_all(chunks, AXIS, 0, 0)  19.6 us
    all_to_all x1, waiting for transfers between devices, shards(): sums = lax.all_to_all(sums, AXIS, 0, 0)  6.4 us
    pallas_call x1, Pallas kernels, shards(): pl.pallas_call(grade_kernel, out_shape=(jax.ShapeDtypeStruct((count, 2, c...  4.81 us
    all_to_all x1, starting transfers between devices, shards(): sums = lax.all_to_all(sums, AXIS, 0, 0)  3.52 us
    pallas_call x1, Pallas kernels, shards(): pl.pallas_call(functools.partial(moment_kernel, columns), out_shape=(jax....  3.2 us
    unnamed x7, local copies, waits for them, and re-layouts  2.63 us
    pallas_call x1, Pallas kernels, shards(): pl.pallas_call(functools.partial(combine_kernel, columns), out_shape=jax....  2.42 us
    ppermute x1, waiting for transfers between devices, shards(): sibling = lax.ppermute(held[:, 1], AXIS, [(i, i ^ 1) for i in range(count)])  1.33 us
  transfers between devices with their start and end apart: 2, of which 2 were waited for; matrix products, arithmetic and copies ran while one was open for 0% of the time, Pallas kernels for 0%

profile of v2, /device:TPU:0, one launch (start us, length us, event | category | flops | bytes accessed | tf_op | source)
XLA Modules:
  0.0 46.3 jit_solution(11340177305684064289)
XLA Ops:
  0.0 1.4 %copy.7.w_in = f32[32,3]{1,0:T(8,128)} copy(f32[32,3]{0,1:T(4,128)} %param.7) | data formatting | bytes 768 | tf_op args[1]
  1.4 4.8 %grade.1 = (bf16[16,2,3,16,128]{4,3,2,1,0:T(8,128)(2,1)}, f32[3,8,128]{2,1,0:T(8,128)}) custom-call(f32[32,3]{1,0:T(8,128)} %copy.7.w_in, f32[32]{0:T(128)} %b_in.1, f32[3,32]{1,0:T(4,128)} %w_out.1, f32[3]{0:T(128)} %b_out.1, f32[3]{0:T(128)} %screen.3, bf16[1,3,32,960]{3,2,1,0:T(8,128)(2,1)} %video.1), custom_call_target="tpu_custom_call" | custom-call | tf_op jit(solution)/shard_map/grade/pallas_call | solution.py:219
  6.2 19.6 %all_to_all.10.held = bf16[16,2,3,16,128]{4,3,2,1,0:T(8,128)(2,1)S(1)} all-to-all(bf16[16,2,3,16,128]{4,3,2,1,0:T(8,128)(2,1)} %get-tuple-element.10), channel_id=1, replica_groups=mesh['video'=2,'tm'=16] {'tm'}, dimensions={0} | all-to-all | bytes 786432 | tf_op jit(solution)/shard_map/all_to_all | solution.py:234
  25.8 0.0 copy-start
  25.8 0.2 collective-permute-start
  26.0 1.3 %collective-permute-done.sibling = bf16[16,3,16,128]{3,2,1,0:T(8,128)(2,1)S(1)} collective-permute-done((bf16[16,3,16,128]{3,2,1,0:T(8,128)(2,1)S(1)}, bf16[16,3,16,128]{3,2,1,0:T(8,128)(2,1)S(1)}, u32[]{:S(2)}, u32[]{:S(2)}) %collective-permute-start) | collective-permute-done | bytes 196640 | tf_op jit(solution)/shard_map/ppermute | solution.py:235
  27.3 0.0 copy-start.1
  27.3 0.0 copy-done
  27.3 0.7 %copy-done.1 = bf16[16,3,16,128]{3,2,1,0:T(8,128)(2,1)} copy-done((bf16[16,3,16,128]{3,2,1,0:T(8,128)(2,1)}, bf16[16,3,16,128]{3,2,1,0:T(8,128)(2,1)S(1)}, u32[]{:S(2)}) %copy-start.1) | copy-done | bytes 196632
  28.0 3.2 %moments.1 = (f32[16,1,128]{2,1,0:T(1,128)}, f32[3,16,16,128]{3,2,1,0:T(8,128)}, f32[3,16,16,128]{3,2,1,0:T(8,128)}) custom-call(f32[1]{0:T(128)} %bitcast.edge, bf16[16,2,3,16,128]{4,3,2,1,0:T(8,128)(2,1)} %copy-done, bf16[16,3,16,128]{3,2,1,0:T(8,128)(2,1)} %copy-done.1, f32[3,8,128]{2,1,0:T(8,128)} %get-tuple-element.11.rho), custom_call_target="tpu_custom_call" | custom-call | tf_op jit(solution)/shard_map/moments/pallas_call | solution.py:238
  31.2 3.5 %all-to-all-start.1 = ((f32[16,1,128]{2,1,0:T(1,128)}), f32[16,1,128]{2,1,0:T(1,128)S(1)}, u32[]{:S(2)}, u32[]{:S(2)}) async-start(f32[16,1,128]{2,1,0:T(1,128)} %get-tuple-element.12), calls=%async_computation.1 | async-start | bytes 16384 | tf_op jit(solution)/shard_map/all_to_all | solution.py:245
  34.7 6.4 %all-to-all-done.1.sums = f32[16,1,128]{2,1,0:T(1,128)S(1)} async-done(((f32[16,1,128]{2,1,0:T(1,128)}), f32[16,1,128]{2,1,0:T(1,128)S(1)}, u32[]{:S(2)}, u32[]{:S(2)}) %all-to-all-start.1) | async-done | bytes 8224 | tf_op jit(solution)/shard_map/all_to_all | solution.py:245
  41.1 0.0 copy-start.2
  41.1 0.6 %copy-done.2 = f32[16,1,128]{2,1,0:T(1,128)} copy-done((f32[16,1,128]{2,1,0:T(1,128)}, f32[16,1,128]{2,1,0:T(1,128)S(1)}, u32[]{:S(2)}) %copy-start.2) | copy-done | bytes 8216
  41.7 2.4 %combine.1 = f32[3,2,16,960]{3,2,1,0:T(8,128)} custom-call(f32[3]{0:T(128)} %screen.3, f32[16,1,128]{2,1,0:T(1,128)} %copy-done.2, bf16[16,2,3,16,128]{4,3,2,1,0:T(8,128)(2,1)} %copy-done, f32[3,16,16,128]{3,2,1,0:T(8,128)} %get-tuple-element.13.first, f32[3,16,16,128]{3,2,1,0:T(8,128)} %get-tuple-element.14.second), custom_call_target="tpu_custom_call" | custom-call | tf_op jit(solution)/shard_map/combine/pallas_call | solution.py:246
  44.1 1.2 %fusion = f32[16,3,2,960]{3,0,2,1:T(8,128)S(1)} fusion(f32[3,2,16,960]{3,2,1,0:T(8,128)} %combine.1, pred[]{:T(512)S(6)} %eq.11), kind=kLoop, calls=%fused_computation.1 | loop fusion | flops 92160 | bytes 737281 | tf_op jit(solution)/shard_map/transpose | solution.py:254
  45.3 1.1 %copy.8 = f32[16,3,2,960]{3,2,1,0:T(2,128)} copy(f32[16,3,2,960]{3,0,2,1:T(8,128)S(1)} %fusion) | data formatting | bytes 737280 | tf_op jit(solution)/shard_map/transpose | solution.py:254
  (1 shorter events, 0.0 us)
Async XLA Ops:
  25.8 1.5 %copy-start = (bf16[16,2,3,16,128]{4,3,2,1,0:T(8,128)(2,1)}, bf16[16,2,3,16,128]{4,3,2,1,0:T(8,128)(2,1)S(1)}, u32[]{:S(2)}) copy-start(bf16[16,2,3,16,128]{4,3,2,1,0:T(8,128)(2,1)S(1)} %all_to_all.10.held) | copy-start | bytes 1179652
  25.8 1.5 %collective-permute-start = (bf16[16,3,16,128]{3,2,1,0:T(8,128)(2,1)S(1)}, bf16[16,3,16,128]{3,2,1,0:T(8,128)(2,1)S(1)}, u32[]{:S(2)}, u32[]{:S(2)}) collective-permute-start(bf16[16,3,16,128]{3,2,1,0:T(8,128)(2,1)S(1)} %slice_bitcast_fusion), channel_id=1, source_target_pairs={{0,1},{1,0},{2,3},{3,2},{4,5},{5,4},{6,7},{7,6},{8,9},{9,8},{10,11... | collective-permute-start | bytes 589832 | tf_op jit(solution)/shard_map/ppermute | solution.py:235
  27.3 0.7 %copy-start.1 = (bf16[16,3,16,128]{3,2,1,0:T(8,128)(2,1)}, bf16[16,3,16,128]{3,2,1,0:T(8,128)(2,1)S(1)}, u32[]{:S(2)}) copy-start(bf16[16,3,16,128]{3,2,1,0:T(8,128)(2,1)S(1)} %collective-permute-done.sibling) | copy-start | bytes 589828
  31.2 9.9 %all-to-all-start.1 = ((f32[16,1,128]{2,1,0:T(1,128)}), f32[16,1,128]{2,1,0:T(1,128)S(1)}, u32[]{:S(2)}, u32[]{:S(2)}) async-start(f32[16,1,128]{2,1,0:T(1,128)} %get-tuple-element.12), calls=%async_computation.1 | async-start | bytes 16384 | tf_op jit(solution)/shard_map/all_to_all | solution.py:245
  41.1 0.6 %copy-start.2 = (f32[16,1,128]{2,1,0:T(1,128)}, f32[16,1,128]{2,1,0:T(1,128)S(1)}, u32[]{:S(2)}) copy-start(f32[16,1,128]{2,1,0:T(1,128)S(1)} %all-to-all-done.1.sums) | copy-start | bytes 24580

commit v3 on v2

v3 whole, which is shorter than its diff:
```python
import functools

import jax
import jax.numpy as jnp
from jax import lax
from jax.experimental import pallas as pl
from jax.experimental.pallas import tpu as pltpu
from jax.sharding import PartitionSpec as P

BLOCKS = 8
LANES = 128
AXIS = "tm"


def lanes_of(shape):
    return lax.broadcasted_iota(jnp.int32, shape, len(shape) - 1)


def three_parts(values, lane):
    high = values.astype(jnp.bfloat16).astype(jnp.float32)
    rest = values - high
    middle = rest.astype(jnp.bfloat16).astype(jnp.float32)
    third = LANES // 4
    return jnp.where(lane < third, high, jnp.where(lane < 2 * third, middle, rest - middle))


def grade_kernel(
    w_in_at, b_in_at, w_out_at, b_out_at, screen_at, video_at, chunks, rho, sigma,
    w_in, b_in, w_out, b_out, screen, video, arrived, graded, blocks, first, second,
):
    copies = [
        pltpu.make_async_copy(source, to, arrived.at[i])
        for i, (source, to) in enumerate(
            [
                (w_in_at, w_in), (b_in_at, b_in), (w_out_at, w_out),
                (b_out_at, b_out), (screen_at, screen), (video_at, video),
            ]
        )
    ]
    for copy in copies:
        copy.start()
    for copy in copies:
        copy.wait()
    channels, rows, columns = video.shape[1:]
    units = b_in.shape[0]
    across = graded.shape[2]
    width = columns // BLOCKS
    halo = (LANES - width) // 2
    dests = chunks.shape[0]

    tile = (8, LANES)
    lane = lanes_of(tile)
    part = lane % (LANES // 4)
    row = lax.broadcasted_iota(jnp.int32, tile, 0)
    used = lane < 3 * (LANES // 4)
    picks = [jnp.where(used & (part == 8 * c + row), 0.5, 0.0) for c in range(channels)]
    ones = jnp.where(used & (part == 8 * channels), 0.5, 0.0)
    for j in range(units):
        values = ones * b_in[j]
        for c in range(channels):
            values = values + picks[c] * w_in[c, j]
            second[c, j] = jnp.full(tile, w_out[c, j])
        first[8 * j : 8 * j + 8] = three_parts(values, lane)
    layer = first[...].astype(jnp.bfloat16)

    span = across // 2

    def grade(step, _):
        top = pl.multiple_of(step * 16, 16)
        for start in range(0, across, span):
            count = min(span, columns - start)
            taken = []
            for c in range(channels):
                values = video[0, c, pl.ds(top, 16), start : start + count].astype(jnp.float32)
                if count < span:
                    empty = jnp.zeros((16, span - count), jnp.float32)
                    values = jnp.concatenate([values, empty], axis=1)
                taken.append(values)
            for r in (0, 8):
                pixels = [values[r : r + 8] for values in taken]
                group = jnp.concatenate(pixels + [jnp.ones((8, span), jnp.float32)], axis=0)
                group = group.astype(jnp.bfloat16)
                group = jnp.concatenate([group] * 3 + [jnp.zeros_like(group)], axis=0)
                half = jnp.dot(layer, group, preferred_element_type=jnp.float32)
                total = [pixels[c] + b_out[c] for c in range(channels)]
                for j in range(units):
                    h = half[8 * j : 8 * j + 8]
                    unit = h + h * jnp.tanh(h)
                    for c in range(channels):
                        total[c] = total[c] + jnp.tile(second[c, j], (1, span // LANES)) * unit
                inside = start + lanes_of((8, span)) < columns
                for c in range(channels):
                    graded[c, pl.ds(top + r, 8), start : start + span] = jnp.where(
                        inside, total[c], 0.0
                    )
        return 0

    lax.fori_loop(0, rows // 16, grade, 0)

    row = lax.broadcasted_iota(jnp.int32, (rows, across), 0)
    inside = lanes_of((rows, across)) < columns
    weight = jnp.full((1, LANES), 1.0, jnp.float32)
    for c in range(channels):
        weight = jnp.where(lane[:1] == c, 6.0 + screen[c], weight)
        g = graded[c]
        above = jnp.where(row == 0, 0.0, pltpu.roll(g, 1, 0))
        below = jnp.where(row == rows - 1, 0.0, pltpu.roll(g, rows - 1, 0))
        beside = pltpu.roll(g, 1, 1) + pltpu.roll(g, across - 1, 1)
        target = (screen[c] + 4.0) * g - (above + below + beside)
        target = jnp.where(inside, target, 0.0).astype(jnp.bfloat16).astype(jnp.float32)
        for top in range(0, rows, 8):
            band = target[top : top + 8]
            parts = []
            for s in range(BLOCKS):
                start = s * width - halo
                v, off = start // LANES, start % LANES
                low = jnp.zeros(tile, jnp.float32)
                if v >= 0:
                    low = pltpu.roll(band[:, v * LANES : (v + 1) * LANES], (LANES - off) % LANES, 1)
                high = pltpu.roll(band[:, (v + 1) * LANES : (v + 2) * LANES], LANES - off, 1)
                parts.append(jnp.where(lane < LANES - off, low, high))
            blocks[c, top : top + 8] = jnp.swapaxes(jnp.stack(parts, axis=0), 0, 1)
    sigma[...] = weight

    for c in range(channels):
        field = [blocks[c, r] for r in range(rows)]
        for _ in range(2):
            field = [
                sum(field[i] for i in (r - 1, r + 1) if 0 <= i < rows) for r in range(rows)
            ]
        total = field[0] * field[1]
        for r in range(1, rows - 1):
            total = total + field[r] * field[r + 1]
        rho[c] = total + total
        zero = jnp.zeros((BLOCKS, LANES), jnp.float32)

        def line(r):
            return blocks[c, r] if 0 <= r < rows else zero

        for d in range(dests):
            if d % 2 == 0:
                order = [2 * d - 2, 2 * d - 1, 2 * d, 2 * d + 1]
            else:
                order = [2 * d + 3, 2 * d + 2, 2 * d + 1, 2 * d]
            for p in range(2):
                pair = jnp.concatenate([line(order[2 * p]), line(order[2 * p + 1])], axis=0)
                chunks[d, p, c] = pair.astype(jnp.bfloat16)


def within(field, mask):
    zero = jnp.zeros_like(field[:1])
    frames = jnp.concatenate([field[1:], zero], axis=0) + jnp.concatenate([zero, field[:-1]], axis=0)
    beside = pltpu.roll(field, 1, 2) + pltpu.roll(field, LANES - 1, 2)
    return frames + jnp.where(mask, beside, 0.0)


def moment_kernel(columns, place, held, sibling, rho, sums, first, second):
    frames, _, channels = held.shape[:3]
    width = columns // BLOCKS
    halo = (LANES - width) // 2
    shape = (frames, 2 * BLOCKS, LANES)
    lane = lanes_of(shape)
    column = (lax.broadcasted_iota(jnp.int32, shape, 1) % BLOCKS) * width - halo + lane
    mask = (column >= 0) & (column < columns)
    own = lanes_of((2 * BLOCKS, LANES))
    own = (own >= halo) & (own < halo + width)
    inside = place[0]
    out_lane = lanes_of((1, LANES))
    result = jnp.zeros((1, LANES), jnp.float32)
    for c in range(channels):
        far = held[:, 0, c].astype(jnp.float32)
        u0 = held[:, 1, c].astype(jnp.float32)
        near = sibling[:, c].astype(jnp.float32)
        b0, b1 = far[:, :BLOCKS], far[:, BLOCKS:]
        b2, b3 = u0[:, :BLOCKS], u0[:, BLOCKS:]
        b5, b4 = near[:, :BLOCKS], near[:, BLOCKS:]
        u1 = jnp.concatenate([b1 + b3, b2 + b4], axis=1)
        u2 = jnp.concatenate([b0 + inside * b2 + b4, b1 + 2.0 * b3 + b5], axis=1)
        k0 = within(u0, mask)
        k1 = within(u1, mask)
        y = 2.0 * k1 + within(k0, mask)
        y1 = 2.0 * within(u2, mask) + within(k1, mask)
        n1 = u1 + k0
        n2 = u2 + y
        first[c] = n1
        second[c] = n2
        moments = [
            u0 * u0,
            u0 * n1,
            n1 * n1,
            n1 * n2,
            n2 * n2,
            n2 * within(n2, mask) + y * y1 + 2.0 * (y1 * u2),
        ]
        for k, product in enumerate(moments):
            total = jnp.sum(product, axis=0)
            total = total[:BLOCKS] + total[BLOCKS:]
            if k == len(moments) - 1:
                total = total + rho[c]
            total = jnp.where(own[:BLOCKS], total, 0.0)
            total = jnp.sum(total, axis=0, keepdims=True)
            total = jnp.sum(total, axis=1, keepdims=True)
            result = jnp.where(out_lane == BLOCKS * k + c, total, result)
    sums[...] = jnp.broadcast_to(result[None], sums.shape)


def combine_kernel(columns, place, sigma_at, sums, held, first, second, out):
    frames, _, channels = held.shape[:3]
    width = columns // BLOCKS
    halo = (LANES - width) // 2
    lane = lanes_of((1, LANES))
    total = jnp.sum(sums[...], axis=0)
    nu = [total] + [pltpu.roll(total, LANES - BLOCKS * k, 1) for k in range(1, 6)]
    sigma = sigma_at[...]
    g = [sigma * nu[k] - nu[k + 1] for k in range(5)]
    l1 = g[1] / g[0]
    l2 = g[2] / g[0]
    d1 = g[2] - l1 * g[1]
    e = g[3] - l1 * g[2]
    m = e / d1
    d2 = g[4] - l2 * g[2] - m * e
    z0 = nu[0]
    z1 = nu[1] - l1 * z0
    z2 = nu[2] - l2 * z0 - m * z1
    c2 = z2 / d2
    c1 = z1 / d1 - m * c2
    c0 = z0 / g[0] - l1 * c1 - l2 * c2

    tile_lane = lanes_of((8, LANES))
    tiles = -(-columns // LANES)
    mirrored = place[1] > 0.5
    for c in range(channels):
        w0, w1, w2 = (
            jnp.sum(jnp.where(lane == c, w, 0.0), axis=1, keepdims=True)[None] for w in (c0, c1, c2)
        )
        x = w0 * held[:, 1, c].astype(jnp.float32) + w1 * first[c] + w2 * second[c]
        low, high = x[:, :BLOCKS], x[:, BLOCKS:]
        low, high = jnp.where(mirrored, high, low), jnp.where(mirrored, low, high)
        for f in range(0, frames, 4):
            lines = [part[i] for i in range(f, f + 4) for part in (low, high)]
            turned = jnp.swapaxes(jnp.stack(lines, axis=0), 0, 1)
            moved = [pltpu.roll(turned[s], (s * width - halo) % LANES, 1) for s in range(BLOCKS)]
            for t in range(tiles):
                piece = moved[t]
                if t + 1 < BLOCKS:
                    bound = width * (t + 1) - LANES * t
                    piece = jnp.where(tile_lane < bound, moved[t], moved[t + 1])
                count = min(LANES, columns - LANES * t)
                for i in range(4):
                    out[f + i, c, :, LANES * t : LANES * t + count] = piece[
                        2 * i : 2 * i + 2, :count
                    ]


def vmem():
    return pl.BlockSpec(memory_space=pltpu.VMEM)


def params():
    return pltpu.CompilerParams(vmem_limit_bytes=32 << 20)


def shards(video, w_in, b_in, w_out, b_out, screen):
    count, me = lax.axis_size(AXIS), lax.axis_index(AXIS)
    _, channels, rows, columns = video.shape
    units = b_in.shape[0]
    frames = count
    across = -(-columns // LANES) * LANES
    w_in = w_in.T
    operands = (w_in, b_in, w_out, b_out, screen, video)
    local = [pltpu.SMEM(a.shape, a.dtype) for a in operands[:-1]]
    chunks, rho, sigma = pl.pallas_call(
        grade_kernel,
        out_shape=(
            jax.ShapeDtypeStruct((count, 2, channels, 2 * BLOCKS, LANES), jnp.bfloat16),
            jax.ShapeDtypeStruct((channels, BLOCKS, LANES), jnp.float32),
            jax.ShapeDtypeStruct((1, LANES), jnp.float32),
        ),
        in_specs=[pl.BlockSpec(memory_space=pltpu.HBM)] * 6,
        out_specs=(vmem(),) * 3,
        scratch_shapes=local
        + [
            pltpu.VMEM(video.shape, video.dtype),
            pltpu.SemaphoreType.DMA((6,)),
            pltpu.VMEM((channels, rows, across), jnp.float32),
            pltpu.VMEM((channels, rows, BLOCKS, LANES), jnp.float32),
            pltpu.VMEM((8 * units, LANES), jnp.float32),
            pltpu.VMEM((channels, units, 8, LANES), jnp.float32),
        ],
        name="grade",
    )(*operands)
    held = lax.all_to_all(chunks, AXIS, 0, 0)
    sibling = lax.ppermute(held[:, 1], AXIS, [(i, i ^ 1) for i in range(count)])
    inside = jnp.where((me == 0) | (me == count - 1), 1.0, 2.0)
    odd = jnp.where(me % 2 == 1, 1.0, 0.0)
    place = jnp.broadcast_to(jnp.stack([inside, odd])[:, None, None], (2, BLOCKS, LANES))
    field = jax.ShapeDtypeStruct((channels, frames, 2 * BLOCKS, LANES), jnp.float32)
    sums, first, second = pl.pallas_call(
        functools.partial(moment_kernel, columns),
        out_shape=(jax.ShapeDtypeStruct((count, 1, LANES), jnp.float32), field, field),
        in_specs=[vmem()] * 4,
        out_specs=(vmem(),) * 3,
        compiler_params=params(),
        name="moments",
    )(place, held, sibling, rho)
    sums = lax.all_to_all(sums, AXIS, 0, 0)
    return pl.pallas_call(
        functools.partial(combine_kernel, columns),
        out_shape=jax.ShapeDtypeStruct((frames, channels, 2, columns), jnp.float32),
        in_specs=[vmem()] * 6,
        out_specs=vmem(),
        compiler_params=params(),
        name="combine",
    )(place, sigma, sums, held, first, second)


def solution(mesh):
    in_specs = (P(("video", AXIS), None, None, None), P(), P(), P(), P(), P())
    out_specs = P("video", None, AXIS, None)
    return jax.shard_map(shards, mesh=mesh, in_specs=in_specs, out_specs=out_specs, check_vma=False)
```

time: 46.7 us -> 38.7 us (0.83)
  blocking collectives: 19.6 us -> 29.3 us
  waiting for transfers between devices: 7.72 us -> 1.25 us
  starting transfers between devices: 3.7 us -> 0.18 us
  Pallas kernels: 10.4 us -> 6.91 us
  local copies, waits for them, and re-layouts: 3.69 us -> 0.68 us
  other arithmetic: 1.16 us -> 0.07 us
    all_to_all x0 -> x1, blocking collectives: none -> 9.72 us  [shards(): sums = lax.all_to_all(sums, AXIS, 0, 0)]
    all_to_all x1 -> x0, waiting for transfers between devices: 6.4 us -> none  [shards(): sums = lax.all_to_all(sums, AXIS, 0, 0)]
    all_to_all x1 -> x0, starting transfers between devices: 3.52 us -> none  [shards(): sums = lax.all_to_all(sums, AXIS, 0, 0)]
    unnamed x7 -> x4, local copies, waits for them, and re-layouts: 2.63 us -> 0.6 us
    pallas_call x1, Pallas kernels: 3.2 us -> 1.53 us  [shards(): pl.pallas_call(functools.partial(moment_kernel, columns), out_shape=(jax....]
    pallas_call x1, Pallas kernels: 2.42 us -> 1.2 us  [shards(): pl.pallas_call(functools.partial(combine_kernel, columns), out_shape=jax....]
    transpose x1 -> x0, other arithmetic: 1.16 us -> none  [shards(): return out.transpose(2, 0, 1, 3)]
    transpose x1 -> x0, local copies, waits for them, and re-layouts: 1.05 us -> none  [shards(): return out.transpose(2, 0, 1, 3)]
  transfers between devices with their start and end apart: 2 -> 1, of which waited for: 2 -> 1; matrix products, arithmetic and copies ran while one was open for 0% -> 0% of each run, Pallas kernels for 0% -> 0%
where the time goes in v3:
time: 38.7 us; the launch traced here: 38.4 us
  blocking collectives  29.3 us (76%)
  Pallas kernels  6.91 us (18%)
  waiting for transfers between devices  1.25 us (3%)
  local copies, waits for them, and re-layouts  0.68 us (2%)
    all_to_all x1, blocking collectives, shards(): held = lax.all_to_all(chunks, AXIS, 0, 0)  19.6 us
    all_to_all x1, blocking collectives, shards(): sums = lax.all_to_all(sums, AXIS, 0, 0)  9.72 us
    pallas_call x1, Pallas kernels, shards(): pl.pallas_call(grade_kernel, out_shape=(jax.ShapeDtypeStruct((count, 2, c...  4.19 us
    pallas_call x1, Pallas kernels, shards(): pl.pallas_call(functools.partial(moment_kernel, columns), out_shape=(jax....  1.53 us
    ppermute x1, waiting for transfers between devices, shards(): sibling = lax.ppermute(held[:, 1], AXIS, [(i, i ^ 1) for i in range(count)])  1.25 us
    pallas_call x1, Pallas kernels, shards(): pl.pallas_call(functools.partial(combine_kernel, columns), out_shape=jax....  1.2 us
  transfers between devices with their start and end apart: 1, of which 1 were waited for; matrix products, arithmetic and copies ran while one was open for 0% of the time, Pallas kernels for 0%

profile of v3, /device:TPU:0, one launch (start us, length us, event | category | flops | bytes accessed | tf_op | source)
XLA Modules:
  0.0 38.4 jit_solution(18086705178489158784)
XLA Ops:
  0.0 4.2 %grade.1 = (bf16[16,2,3,16,128]{4,3,2,1,0:T(8,128)(2,1)}, f32[3,8,128]{2,1,0:T(8,128)}, f32[1,128]{1,0:T(1,128)}) custom-call(f32[3,32]{1,0:T(4,128)} %bitcast.5, f32[32]{0:T(128)} %b_in_at.1, f32[3,32]{1,0:T(4,128)} %w_out_at.1, f32[3]{0:T(128)} %b_out_at.1, f32[3]{0:T(128)} %screen_at.1, bf16[1,3,32,960]{3,2,1,0:T(8,128)(2,1)} %video_at.1), custom_call_target="tpu_custom_call" | custom-call | tf_op jit(solution)/shard_map/grade/pallas_call | solution.py:272
  4.2 19.6 %all_to_all.10.held = bf16[16,2,3,16,128]{4,3,2,1,0:T(8,128)(2,1)S(1)} all-to-all(bf16[16,2,3,16,128]{4,3,2,1,0:T(8,128)(2,1)} %get-tuple-element.12), channel_id=1, replica_groups=mesh['video'=2,'tm'=16] {'tm'}, dimensions={0} | all-to-all | bytes 786432 | tf_op jit(solution)/shard_map/all_to_all | solution.py:292
  23.8 0.2 collective-permute-start
  24.0 0.0 copy-start
  24.0 0.1 pad_maximum_fusion
  24.1 1.2 %collective-permute-done.sibling = bf16[16,3,16,128]{3,2,1,0:T(8,128)(2,1)S(1)} collective-permute-done((bf16[16,3,16,128]{3,2,1,0:T(8,128)(2,1)S(1)}, bf16[16,3,16,128]{3,2,1,0:T(8,128)(2,1)S(1)}, u32[]{:S(2)}, u32[]{:S(2)}) %collective-permute-start) | collective-permute-done | bytes 196640 | tf_op jit(solution)/shard_map/ppermute | solution.py:293
  25.3 0.1 broadcast_in_dim.2.place
  25.4 0.0 copy-done
  25.4 1.5 %moments.1 = (f32[16,1,128]{2,1,0:T(1,128)S(1)}, f32[3,16,16,128]{3,2,1,0:T(8,128)S(1)}, f32[3,16,16,128]{3,2,1,0:T(8,128)S(1)}) custom-call(f32[2,8,128]{2,1,0:T(8,128)S(1)} %broadcast_in_dim.2.place, bf16[16,2,3,16,128]{4,3,2,1,0:T(8,128)(2,1)S(1)} %all_to_all.10.held, bf16[16,3,16,128]{3,2,1,0:T(8,128)(2,1)S(1)} %collective-permute-done.sibling, ...), custom_call_target="tpu_custom_call" | custom-call | tf_op jit(solution)/shard_map/moments/pallas_call | solution.py:298
  26.9 9.7 %all_to_all.11.sums = f32[16,1,128]{2,1,0:T(1,128)S(1)} all-to-all(f32[16,1,128]{2,1,0:T(1,128)S(1)} %get-tuple-element.14), channel_id=1, replica_groups=mesh['video'=2,'tm'=16] {'tm'}, dimensions={0} | all-to-all | bytes 16384 | tf_op jit(solution)/shard_map/all_to_all | solution.py:306
  36.6 0.0 copy-start.1
  36.6 0.6 %copy-done.1 = f32[1,128]{1,0:T(1,128)S(1)} copy-done((f32[1,128]{1,0:T(1,128)S(1)}, f32[1,128]{1,0:T(1,128)}, u32[]{:S(2)}) %copy-start.1) | copy-done | bytes 536
  37.2 1.2 %combine.1 = f32[16,3,2,960]{3,2,1,0:T(2,128)} custom-call(f32[2,8,128]{2,1,0:T(8,128)S(1)} %broadcast_in_dim.2.place, f32[1,128]{1,0:T(1,128)S(1)} %copy-done.1, f32[16,1,128]{2,1,0:T(1,128)S(1)} %all_to_all.11.sums, bf16[16,2,3,16,128]{4,3,2,1,0:T(8,128)(2,1)S(1)} %all_to_all.10.held, f32[3,16,16,128]{3,2,1,0:T(8,128)S(1)} %get-tuple-element.15.first, ...), custom_call_target="tpu_custom_call" | custom-call | tf_op jit(solution)/shard_map/combine/pallas_call | solution.py:307
  (1 shorter events, 0.0 us)
Async XLA Ops:
  23.8 1.5 %collective-permute-start = (bf16[16,3,16,128]{3,2,1,0:T(8,128)(2,1)S(1)}, bf16[16,3,16,128]{3,2,1,0:T(8,128)(2,1)S(1)}, u32[]{:S(2)}, u32[]{:S(2)}) collective-permute-start(bf16[16,3,16,128]{3,2,1,0:T(8,128)(2,1)S(1)} %slice_bitcast_fusion), channel_id=1, source_target_pairs={{0,1},{1,0},{2,3},{3,2},{4,5},{5,4},{6,7},{7,6},{8,9},{9,8},{10,11... | collective-permute-start | bytes 589832 | tf_op jit(solution)/shard_map/ppermute | solution.py:293
  24.0 1.4 %copy-start = (f32[3,8,128]{2,1,0:T(8,128)S(1)}, f32[3,8,128]{2,1,0:T(8,128)}, u32[]{:S(2)}) copy-start(f32[3,8,128]{2,1,0:T(8,128)} %get-tuple-element.13.rho) | copy-start | bytes 36868
  36.6 0.6 %copy-start.1 = (f32[1,128]{1,0:T(1,128)S(1)}, f32[1,128]{1,0:T(1,128)}, u32[]{:S(2)}) copy-start(f32[1,128]{1,0:T(1,128)} %get-tuple-element.11.sigma_at) | copy-start | bytes 1540

commit v4 on v3

v4 whole, which is shorter than its diff:
```python
import functools

import jax
import jax.numpy as jnp
from jax import lax
from jax.experimental import pallas as pl
from jax.experimental.pallas import tpu as pltpu
from jax.sharding import PartitionSpec as P

BLOCKS = 8
LANES = 128
TILE = (8, LANES)
AXIS = "tm"


def lanes_of(shape):
    return lax.broadcasted_iota(jnp.int32, shape, len(shape) - 1)


def sublanes_of(shape):
    return lax.broadcasted_iota(jnp.int32, shape, len(shape) - 2)


def turn_pairs(tiles):
    sublane = sublanes_of(TILE)
    lower, even = sublane < 4, sublane % 4 < 2
    mixed = []
    for i in (0, 1):
        a, b = tiles[i], tiles[i + 2]
        mixed.append(
            (jnp.where(lower, a, pltpu.roll(b, 4, 0)), jnp.where(lower, pltpu.roll(a, 4, 0), b))
        )
    turned = []
    for i in (0, 1):
        a, b = mixed[0][i], mixed[1][i]
        turned.append(jnp.where(even, a, pltpu.roll(b, 2, 0)))
        turned.append(jnp.where(even, pltpu.roll(a, 6, 0), b))
    return turned


def three_parts(values, lane):
    high = values.astype(jnp.bfloat16).astype(jnp.float32)
    rest = values - high
    middle = rest.astype(jnp.bfloat16).astype(jnp.float32)
    third = LANES // 4
    return jnp.where(lane < third, high, jnp.where(lane < 2 * third, middle, rest - middle))


def grade_kernel(
    w_in_at, b_in_at, w_out_at, b_out_at, screen_at, video_at, chunks, extra,
    w_in, b_in, w_out, b_out, screen, video, arrived, sent,
    graded, tiles, first, second, ready, notes,
):
    channels, rows, columns = video.shape[1:]
    units = b_in.shape[0]
    across = graded.shape[2]
    width = columns // BLOCKS
    halo = (LANES - width) // 2
    chips = chunks.shape[0] // 2
    weights = [
        pltpu.make_async_copy(source, to, arrived.at[i])
        for i, (source, to) in enumerate(
            [
                (w_in_at, w_in), (b_in_at, b_in), (w_out_at, w_out),
                (b_out_at, b_out), (screen_at, screen),
            ]
        )
    ]
    pixels_in = pltpu.make_async_copy(video_at, video, arrived.at[5])
    pixels_in.start()
    for copy in weights:
        copy.start()
    for copy in weights:
        copy.wait()

    lane, sublane = lanes_of(TILE), sublanes_of(TILE)
    part = lane % (LANES // 4)
    used = lane < 3 * (LANES // 4)
    picks = [jnp.where(used & (part == 8 * c + sublane), 0.5, 0.0) for c in range(channels)]
    ones = jnp.where(used & (part == 8 * channels), 0.5, 0.0)
    mix = [[jnp.zeros(TILE, jnp.float32) for _ in range(channels + 1)] for _ in range(channels)]
    for j in range(units):
        into = [jnp.full(TILE, w_in[c, j]) for c in range(channels)] + [jnp.full(TILE, b_in[j])]
        values = ones * into[channels]
        for c in range(channels):
            values = values + picks[c] * into[c]
        first[8 * j : 8 * j + 8] = three_parts(values, lane)
        for c in range(channels):
            out = jnp.full(TILE, w_out[c, j])
            second[c, j] = out
            for k in range(channels + 1):
                mix[c][k] = mix[c][k] + (0.5 * out) * into[k]
    for c in range(channels):
        mix[c][c] = mix[c][c] + 1.0
        mix[c][channels] = mix[c][channels] + b_out[c]
    layer = first[...].astype(jnp.bfloat16)
    pixels_in.wait()

    span = across // 2
    times = span // LANES

    def wide(tile):
        return jnp.tile(tile, (1, times))

    def grade(step, _):
        top = pl.multiple_of(step * 16, 16)
        for start in range(0, across, span):
            count = min(span, columns - start)
            taken = []
            for c in range(channels):
                values = video[0, c, pl.ds(top, 16), start : start + count].astype(jnp.float32)
                if count < span:
                    empty = jnp.zeros((16, span - count), jnp.float32)
                    values = jnp.concatenate([values, empty], axis=1)
                taken.append(values)
            for r in (0, 8):
                pixels = [values[r : r + 8] for values in taken]
                group = jnp.concatenate(pixels + [jnp.ones((8, span), jnp.float32)], axis=0)
                group = group.astype(jnp.bfloat16)
                group = jnp.concatenate([group] * 3 + [jnp.zeros_like(group)], axis=0)
                half = jnp.dot(layer, group, preferred_element_type=jnp.float32)
                total = []
                for c in range(channels):
                    linear = wide(mix[c][channels])
                    for k in range(channels):
                        linear = linear + wide(mix[c][k]) * pixels[k]
                    total.append(linear)
                for j in range(units):
                    h = half[8 * j : 8 * j + 8]
                    unit = h * jnp.tanh(h)
                    for c in range(channels):
                        total[c] = total[c] + wide(second[c, j]) * unit
                inside = start + lanes_of((8, span)) < columns
                for c in range(channels):
                    graded[c, pl.ds(top + r, 8), start : start + span] = jnp.where(
                        inside, total[c], 0.0
                    )
        return 0

    lax.fori_loop(0, rows // 16, grade, 0)

    line = sublanes_of((rows, across))
    inside = lanes_of((rows, across)) < columns
    upper = sublane % 2 == 0
    zero = jnp.zeros(TILE, jnp.float32)
    sigma = jnp.full(TILE, 1.0, jnp.float32)
    copies = []
    for c in range(channels):
        sigma = jnp.where(lane == c, 6.0 + screen[c], sigma)
        g = graded[c]
        above = jnp.where(line == 0, 0.0, pltpu.roll(g, 1, 0))
        below = jnp.where(line == rows - 1, 0.0, pltpu.roll(g, rows - 1, 0))
        beside = pltpu.roll(g, 1, 1) + pltpu.roll(g, across - 1, 1)
        target = (screen[c] + 4.0) * g - (above + below + beside)
        target = jnp.where(inside, target, 0.0).astype(jnp.bfloat16).astype(jnp.float32)
        for top in range(0, rows, 8):
            band = target[top : top + 8]
            parts = []
            for s in range(BLOCKS):
                start = s * width - halo
                v, off = start // LANES, start % LANES
                low = zero
                if v >= 0:
                    low = pltpu.roll(band[:, v * LANES : (v + 1) * LANES], (LANES - off) % LANES, 1)
                high = pltpu.roll(band[:, (v + 1) * LANES : (v + 2) * LANES], LANES - off, 1)
                parts.append(jnp.where(lane < LANES - off, low, high))
            for side in range(2):
                for k, tile in enumerate(turn_pairs(parts[4 * side : 4 * side + 4])):
                    tiles[c, side, top // 2 + k] = tile
        pairs = rows // 2
        for side in range(2):

            def pair(k):
                return tiles[c, side, k] if 0 <= k < pairs else zero

            for q in range(chips):
                for p in range(2):
                    k = 2 * q - 1 + 2 * p
                    both = jnp.concatenate([pair(k), pair(k + 1)], axis=0)
                    ready[c, 2 * q + side, p] = both.astype(jnp.bfloat16)
        copies.append(pltpu.make_async_copy(ready.at[c], chunks.at[:, c], sent.at[c]))
        copies[-1].start()

    for c in range(channels):
        total = zero
        for side in range(2):
            field = [tiles[c, side, k] for k in range(pairs)]
            twice = []
            for k in range(pairs):
                beyond = zero
                if k > 0:
                    beyond = beyond + field[k - 1]
                if k < pairs - 1:
                    beyond = beyond + field[k + 1]
                own = 2.0 * field[k]
                if k == 0:
                    own = jnp.where(upper, field[k], own)
                if k == pairs - 1:
                    own = jnp.where(upper, own, field[k])
                twice.append(own + beyond)
            for k in range(pairs):
                after = pltpu.roll(twice[k + 1], 1, 0) if k < pairs - 1 else zero
                total = total + twice[k] * jnp.where(upper, pltpu.roll(twice[k], 7, 0), after)
        notes[c] = total + total
    notes[channels] = sigma
    copies.append(pltpu.make_async_copy(notes, extra, sent.at[channels]))
    copies[-1].start()
    for copy in copies:
        copy.wait()


def within(field, mask):
    zero = jnp.zeros_like(field[:1])
    frames = jnp.concatenate([field[1:], zero], axis=0) + jnp.concatenate([zero, field[:-1]], axis=0)
    beside = pltpu.roll(field, 1, 2) + pltpu.roll(field, LANES - 1, 2)
    return frames + jnp.where(mask, beside, 0.0)


def moment_kernel(columns, place, held, extra, sums, kept, given, sigma):
    frames, channels = held.shape[:2]
    width = columns // BLOCKS
    halo = (LANES - width) // 2
    odd = place[2] > 0.5
    lane, sublane = lanes_of(TILE), sublanes_of(TILE)
    block = sublane // 2 + jnp.where(odd, BLOCKS // 2, 0)
    column = block * width - halo + lane
    mask = ((column >= 0) & (column < columns))[None]
    own = (lane >= halo) & (lane < halo + width)
    upper = (sublane % 2 == 0)[None]
    top = jnp.where(upper, place[0][None], 2.0)
    bottom = jnp.where(upper, 2.0, place[1][None])
    out_lane = lanes_of((1, LANES))
    result = jnp.zeros((1, LANES), jnp.float32)
    for c in range(channels):
        halves = [held[:, c, p].astype(jnp.float32) for p in range(2)]
        b = [halves[0][:, :8], halves[0][:, 8:], halves[1][:, :8], halves[1][:, 8:]]
        between = [b[i] + b[i + 1] for i in range(3)]
        totals = [jnp.zeros(TILE, jnp.float32) for _ in range(6)]
        totals[5] = extra[c]
        sides = []
        for i in (1, 2):
            u0 = b[i]
            u1 = jnp.where(upper, pltpu.roll(between[i - 1], 7, 1), pltpu.roll(between[i], 1, 1))
            u2 = b[i - 1] + (top if i == 1 else bottom) * u0 + b[i + 1]
            k0 = within(u0, mask)
            k1 = within(u1, mask)
            y = 2.0 * k1 + within(k0, mask)
            y1 = 2.0 * within(u2, mask) + within(k1, mask)
            n1 = u1 + k0
            n2 = u2 + y
            sides.append((u0, n1, n2))
            products = [
                u0 * u0,
                u0 * n1,
                n1 * n1,
                n1 * n2,
                n2 * n2,
                n2 * within(n2, mask) + y * y1 + 2.0 * (y1 * u2),
            ]
            for k, product in enumerate(products):
                totals[k] = totals[k] + jnp.sum(product, axis=0)
        for k in range(3):
            kept[k, c] = jnp.where(odd[None], sides[1][k], sides[0][k])
            given[k, c] = jnp.where(odd[None], sides[0][k], sides[1][k])
        for k, total in enumerate(totals):
            total = jnp.where(own, total, 0.0)
            total = jnp.sum(total, axis=0, keepdims=True)
            total = jnp.sum(total, axis=1, keepdims=True)
            result = jnp.where(out_lane == 8 * k + c, total, result)
    sums[...] = jnp.broadcast_to(result[None], sums.shape)
    sigma[...] = extra[channels]


def combine_kernel(columns, place, sigma_at, sums, kept, taken, out):
    channels, frames = kept.shape[1:3]
    width = columns // BLOCKS
    halo = (LANES - width) // 2
    lane = lanes_of((1, LANES))
    total = jnp.sum(sums[...], axis=0)
    nu = [total] + [pltpu.roll(total, LANES - 8 * k, 1) for k in range(1, 6)]
    sigma = sigma_at[:1]
    g = [sigma * nu[k] - nu[k + 1] for k in range(5)]
    l1 = g[1] / g[0]
    l2 = g[2] / g[0]
    d1 = g[2] - l1 * g[1]
    e = g[3] - l1 * g[2]
    m = e / d1
    d2 = g[4] - l2 * g[2] - m * e
    z0 = nu[0]
    z1 = nu[1] - l1 * z0
    z2 = nu[2] - l2 * z0 - m * z1
    c2 = z2 / d2
    c1 = z1 / d1 - m * c2
    c0 = z0 / g[0] - l1 * c1 - l2 * c2

    tile_lane = lanes_of(TILE)
    tiles = -(-columns // LANES)
    odd = place[2] > 0.5
    for c in range(channels):
        w = [jnp.sum(jnp.where(lane == c, w, 0.0), axis=1, keepdims=True) for w in (c0, c1, c2)]
        for f in range(0, frames, 4):
            mine, other = [], []
            for i in range(f, f + 4):
                x = w[0] * kept[0, c, i] + w[1] * kept[1, c, i] + w[2] * kept[2, c, i]
                z = w[0] * taken[0, c, i] + w[1] * taken[1, c, i] + w[2] * taken[2, c, i]
                mine.append(jnp.where(odd, z, x))
                other.append(jnp.where(odd, x, z))
            turned = turn_pairs(mine) + turn_pairs(other)
            moved = [pltpu.roll(turned[s], (s * width - halo) % LANES, 1) for s in range(BLOCKS)]
            for t in range(tiles):
                piece = moved[t]
                if t + 1 < BLOCKS:
                    bound = width * (t + 1) - LANES * t
                    piece = jnp.where(tile_lane < bound, moved[t], moved[t + 1])
                count = min(LANES, columns - LANES * t)
                for i in range(4):
                    out[f + i, c, :, LANES * t : LANES * t + count] = piece[
                        2 * i : 2 * i + 2, :count
                    ]


def vmem():
    return pl.BlockSpec(memory_space=pltpu.VMEM)


def hbm():
    return pl.BlockSpec(memory_space=pltpu.HBM)


def params():
    return pltpu.CompilerParams(vmem_limit_bytes=32 << 20)


def shards(video, w_in, b_in, w_out, b_out, screen):
    count, me = lax.axis_size(AXIS), lax.axis_index(AXIS)
    _, channels, rows, columns = video.shape
    units = b_in.shape[0]
    frames = count
    across = -(-columns // LANES) * LANES
    operands = (w_in.T, b_in, w_out, b_out, screen, video)
    chunk = (channels, 2, 16, LANES)
    chunks, extra = pl.pallas_call(
        grade_kernel,
        out_shape=(
            jax.ShapeDtypeStruct((count,) + chunk, jnp.bfloat16),
            jax.ShapeDtypeStruct((channels + 1,) + TILE, jnp.float32),
        ),
        in_specs=[hbm()] * 6,
        out_specs=(hbm(),) * 2,
        scratch_shapes=[pltpu.SMEM(a.shape, a.dtype) for a in operands[:-1]]
        + [
            pltpu.VMEM(video.shape, video.dtype),
            pltpu.SemaphoreType.DMA((6,)),
            pltpu.SemaphoreType.DMA((channels + 1,)),
            pltpu.VMEM((channels, rows, across), jnp.float32),
            pltpu.VMEM((channels, 2, rows // 2) + TILE, jnp.float32),
            pltpu.VMEM((8 * units, LANES), jnp.float32),
            pltpu.VMEM((channels, units) + TILE, jnp.float32),
            pltpu.VMEM((channels, count) + chunk[1:], jnp.bfloat16),
            pltpu.VMEM((channels + 1,) + TILE, jnp.float32),
        ],
        name="grade",
    )(*operands)
    held = lax.all_to_all(chunks, AXIS, 0, 0)
    ends = [jnp.where(me // 2 == e, 1.0, 2.0) for e in (0, count // 2 - 1)]
    place = jnp.stack(ends + [jnp.where(me % 2 == 1, 1.0, 0.0)])
    place = jnp.broadcast_to(place[:, None, None], (3,) + TILE)
    fields = jax.ShapeDtypeStruct((3, channels, frames) + TILE, jnp.float32)
    sums, kept, given, sigma = pl.pallas_call(
        functools.partial(moment_kernel, columns),
        out_shape=(
            jax.ShapeDtypeStruct((count, 1, LANES), jnp.float32),
            fields,
            fields,
            jax.ShapeDtypeStruct(TILE, jnp.float32),
        ),
        in_specs=[vmem()] * 3,
        out_specs=(vmem(),) * 4,
        compiler_params=params(),
        name="moments",
    )(place, held, extra)
    taken = lax.ppermute(given, AXIS, [(i, i ^ 1) for i in range(count)])
    sums = lax.all_to_all(sums, AXIS, 0, 0)
    return pl.pallas_call(
        functools.partial(combine_kernel, columns),
        out_shape=jax.ShapeDtypeStruct((frames, channels, 2, columns), jnp.float32),
        in_specs=[vmem()] * 5,
        out_specs=vmem(),
        compiler_params=params(),
        name="combine",
    )(place, sigma, sums, kept, taken)


def solution(mesh):
    in_specs = (P(("video", AXIS), None, None, None), P(), P(), P(), P(), P())
    out_specs = P("video", None, AXIS, None)
    return jax.shard_map(shards, mesh=mesh, in_specs=in_specs, out_specs=out_specs, check_vma=False)
```

time: 38.7 us -> 37 us (0.956)
  blocking collectives: 29.3 us -> 9.9 us
  waiting for transfers between devices: 1.25 us -> 12.1 us
  starting transfers between devices: 0.18 us -> 7.52 us
  local copies, waits for them, and re-layouts: 0.68 us -> 0.07 us
    all_to_all x1 -> x0, blocking collectives: 19.6 us -> none  [shards(): held = lax.all_to_all(chunks, AXIS, 0, 0)]
    all_to_all x0 -> x1, waiting for transfers between devices: none -> 12.1 us  [shards(): held = lax.all_to_all(chunks, AXIS, 0, 0)]
    all_to_all x0 -> x1, starting transfers between devices: none -> 7.4 us  [shards(): held = lax.all_to_all(chunks, AXIS, 0, 0)]
    ppermute x1, waiting for transfers between devices: 1.25 us -> 0.01 us  [shards(): taken = lax.ppermute(given, AXIS, [(i, i ^ 1) for i in range(count)])]
    unnamed x4 -> x2, local copies, waits for them, and re-layouts: 0.6 us -> 0.01 us
  transfers between devices with their start and end apart: 1 -> 2, of which waited for: 1 -> 1; matrix products, arithmetic and copies ran while one was open for 0% -> 0% of each run, Pallas kernels for 0% -> 0%
where the time goes in v4:
time: 37 us; the launch traced here: 36.7 us
  waiting for transfers between devices  12.1 us (33%)
  blocking collectives  9.9 us (27%)
  starting transfers between devices  7.52 us (20%)
  Pallas kernels  7.01 us (19%)
    all_to_all x1, waiting for transfers between devices, shards(): held = lax.all_to_all(chunks, AXIS, 0, 0)  12.1 us
    all_to_all x1, blocking collectives, shards(): sums = lax.all_to_all(sums, AXIS, 0, 0)  9.9 us
    all_to_all x1, starting transfers between devices, shards(): held = lax.all_to_all(chunks, AXIS, 0, 0)  7.4 us
    pallas_call x1, Pallas kernels, shards(): pl.pallas_call(grade_kernel, out_shape=(jax.ShapeDtypeStruct((count,) + c...  4.14 us
    pallas_call x1, Pallas kernels, shards(): pl.pallas_call(functools.partial(moment_kernel, columns), out_shape=(jax....  1.68 us
    pallas_call x1, Pallas kernels, shards(): pl.pallas_call(functools.partial(combine_kernel, columns), out_shape=jax....  1.19 us
  transfers between devices with their start and end apart: 2, of which 1 were waited for; matrix products, arithmetic and copies ran while one was open for 0% of the time, Pallas kernels for 0%

profile of v4, /device:TPU:0, one launch (start us, length us, event | category | flops | bytes accessed | tf_op | source)
XLA Modules:
  0.0 36.7 jit_solution(6027904074716494843)
XLA Ops:
  0.0 4.1 %grade.1 = (bf16[16,3,2,16,128]{4,3,2,1,0:T(8,128)(2,1)}, f32[4,8,128]{2,1,0:T(8,128)}) custom-call(f32[3,32]{1,0:T(4,128)} %bitcast.4, f32[32]{0:T(128)} %b_in_at.1, f32[3,32]{1,0:T(4,128)} %w_out_at.1, f32[3]{0:T(128)} %b_out_at.1, f32[3]{0:T(128)} %screen_at.1, bf16[1,3,32,960]{3,2,1,0:T(8,128)(2,1)} %video_at.1), custom_call_target="tpu_custom_call" | custom-call | tf_op jit(solution)/shard_map/grade/pallas_call | solution.py:342
  4.2 7.4 %all-to-all-start = ((bf16[16,3,2,16,128]{4,3,2,1,0:T(8,128)(2,1)}), bf16[16,3,2,16,128]{4,3,2,1,0:T(8,128)(2,1)S(1)}, u32[]{:S(2)}, u32[]{:S(2)}) async-start(bf16[16,3,2,16,128]{4,3,2,1,0:T(8,128)(2,1)} %get-tuple-element.11), calls=%async_computation | async-start | bytes 786432 | tf_op jit(solution)/shard_map/all_to_all | solution.py:364
  11.6 0.0 copy-start
  11.6 0.1 pad_maximum_fusion
  11.7 12.1 %all-to-all-done.held = bf16[16,3,2,16,128]{4,3,2,1,0:T(8,128)(2,1)S(1)} async-done(((bf16[16,3,2,16,128]{4,3,2,1,0:T(8,128)(2,1)}), bf16[16,3,2,16,128]{4,3,2,1,0:T(8,128)(2,1)S(1)}, u32[]{:S(2)}, u32[]{:S(2)}) %all-to-all-start) | async-done | bytes 393248 | tf_op jit(solution)/shard_map/all_to_all | solution.py:364
  23.8 0.1 broadcast_in_dim.2.place
  23.8 0.0 copy-done
  23.8 1.7 %moments.1 = (f32[16,1,128]{2,1,0:T(1,128)S(1)}, f32[3,3,16,8,128]{4,3,2,1,0:T(8,128)S(1)}, f32[3,3,16,8,128]{4,3,2,1,0:T(8,128)S(1)}, f32[8,128]{1,0:T(8,128)S(1)}) custom-call(f32[3,8,128]{2,1,0:T(8,128)S(1)} %broadcast_in_dim.2.place, bf16[16,3,2,16,128]{4,3,2,1,0:T(8,128)(2,1)S(1)} %all-to-all-done.held, f32[4,8,128]{2,1,0:T(8,128)S(1)} %copy-done), custom_call_target="tpu_custom_call" | custom-call | tf_op jit(solution)/shard_map/moments/pallas_call | solution.py:369
  25.5 0.1 collective-permute-start
  25.6 9.9 %all_to_all.10.sums = f32[16,1,128]{2,1,0:T(1,128)S(1)} all-to-all(f32[16,1,128]{2,1,0:T(1,128)S(1)} %get-tuple-element.14), channel_id=1, replica_groups=mesh['video'=2,'tm'=16] {'tm'}, dimensions={0} | all-to-all | bytes 16384 | tf_op jit(solution)/shard_map/all_to_all | solution.py:383
  35.5 0.0 collective-permute-done.taken
  35.5 1.2 %combine.1 = f32[16,3,2,960]{3,2,1,0:T(2,128)} custom-call(f32[3,8,128]{2,1,0:T(8,128)S(1)} %broadcast_in_dim.2.place, f32[8,128]{1,0:T(8,128)S(1)} %get-tuple-element.13.sigma_at, f32[16,1,128]{2,1,0:T(1,128)S(1)} %all_to_all.10.sums, f32[3,3,16,8,128]{4,3,2,1,0:T(8,128)S(1)} %get-tuple-element.15.kept, f32[3,3,16,8,128]{4,3,2,1,0:T(8,128)S(1)} %collective-permute-done.taken), custom_call_target="tpu_custom_call" | custom-call | tf_op jit(solution)/shard_map/combine/pallas_call | solution.py:384
Async XLA Ops:
  4.2 19.6 %all-to-all-start = ((bf16[16,3,2,16,128]{4,3,2,1,0:T(8,128)(2,1)}), bf16[16,3,2,16,128]{4,3,2,1,0:T(8,128)(2,1)S(1)}, u32[]{:S(2)}, u32[]{:S(2)}) async-start(bf16[16,3,2,16,128]{4,3,2,1,0:T(8,128)(2,1)} %get-tuple-element.11), calls=%async_computation | async-start | bytes 786432 | tf_op jit(solution)/shard_map/all_to_all | solution.py:364
  11.6 12.2 %copy-start = (f32[4,8,128]{2,1,0:T(8,128)S(1)}, f32[4,8,128]{2,1,0:T(8,128)}, u32[]{:S(2)}) copy-start(f32[4,8,128]{2,1,0:T(8,128)} %get-tuple-element.12.extra) | copy-start | bytes 49156
  25.5 10.0 %collective-permute-start = (f32[3,3,16,8,128]{4,3,2,1,0:T(8,128)S(1)}, f32[3,3,16,8,128]{4,3,2,1,0:T(8,128)S(1)}, u32[]{:S(2)}, u32[]{:S(2)}) collective-permute-start(f32[3,3,16,8,128]{4,3,2,1,0:T(8,128)S(1)} %get-tuple-element.16), channel_id=1, source_target_pairs={{0,1},{1,0},{2,3},{3,2},{4,5},{5,4},{6,7},{7,6},{8,9},{9,8},{10,11... | collective-permute-start | bytes 1769480 | tf_op jit(solution)/shard_map/ppermute | solution.py:382

commit v5 on v4

--- a/solution.py
+++ b/solution.py
@@ -19,6 +19,10 @@
 
 def sublanes_of(shape):
     return lax.broadcasted_iota(jnp.int32, shape, len(shape) - 2)
+
+
+def first_member(count):
+    return max(count * 3 // 4 - 1, 0)
 
 
 def turn_pairs(tiles):
@@ -177,7 +181,8 @@
                 for p in range(2):
                     k = 2 * q - 1 + 2 * p
                     both = jnp.concatenate([pair(k), pair(k + 1)], axis=0)
-                    ready[c, 2 * q + side, p] = both.astype(jnp.bfloat16)
+                    at = (first_member(2 * chips) - (2 * q + side)) % (2 * chips)
+                    ready[c, at, p] = both.astype(jnp.bfloat16)
         copies.append(pltpu.make_async_copy(ready.at[c], chunks.at[:, c], sent.at[c]))
         copies[-1].start()
 
@@ -232,7 +237,11 @@
     out_lane = lanes_of((1, LANES))
     result = jnp.zeros((1, LANES), jnp.float32)
     for c in range(channels):
-        halves = [held[:, c, p].astype(jnp.float32) for p in range(2)]
+        turn = first_member(frames) + 1
+        halves = [
+            jnp.concatenate([held[turn:, c, p], held[:turn, c, p]], axis=0).astype(jnp.float32)
+            for p in range(2)
+        ]
         b = [halves[0][:, :8], halves[0][:, 8:], halves[1][:, :8], halves[1][:, 8:]]
         between = [b[i] + b[i + 1] for i in range(3)]
         totals = [jnp.zeros(TILE, jnp.float32) for _ in range(6)]
@@ -314,7 +323,7 @@
                     piece = jnp.where(tile_lane < bound, moved[t], moved[t + 1])
                 count = min(LANES, columns - LANES * t)
                 for i in range(4):
-                    out[f + i, c, :, LANES * t : LANES * t + count] = piece[
+                    out[frames - 1 - (f + i), c, :, LANES * t : LANES * t + count] = piece[
                         2 * i : 2 * i + 2, :count
                     ]
 
@@ -361,7 +370,9 @@
         ],
         name="grade",
     )(*operands)
-    held = lax.all_to_all(chunks, AXIS, 0, 0)
+    first = first_member(count)
+    order = [(first - i) % count for i in range(count)]
+    held = lax.all_to_all(chunks, AXIS, 0, 0, axis_index_groups=[order])
     ends = [jnp.where(me // 2 == e, 1.0, 2.0) for e in (0, count // 2 - 1)]
     place = jnp.stack(ends + [jnp.where(me % 2 == 1, 1.0, 0.0)])
     place = jnp.broadcast_to(place[:, None, None], (3,) + TILE)
@@ -380,7 +391,8 @@
         name="moments",
     )(place, held, extra)
     taken = lax.ppermute(given, AXIS, [(i, i ^ 1) for i in range(count)])
-    sums = lax.all_to_all(sums, AXIS, 0, 0)
+    down = list(range(count))[::-1]
+    sums = lax.all_to_all(sums, AXIS, 0, 0, axis_index_groups=[down])
     return pl.pallas_call(
         functools.partial(combine_kernel, columns),
         out_shape=jax.ShapeDtypeStruct((frames, channels, 2, columns), jnp.float32),

time: 37 us -> 32.8 us (0.89)
  waiting for transfers between devices: 12.1 us -> 9.08 us
  blocking collectives: 9.9 us -> 7.89 us
  starting transfers between devices: 7.52 us -> 8.43 us
    all_to_all x1, waiting for transfers between devices: 12.1 us -> 9.08 us  [shards(): held = lax.all_to_all(chunks, AXIS, 0, 0, axis_index_groups=[order])]
    all_to_all x1, blocking collectives: 9.9 us -> 7.89 us  [shards(): sums = lax.all_to_all(sums, AXIS, 0, 0, axis_index_groups=[down])]
    all_to_all x1, starting transfers between devices: 7.4 us -> 7.88 us  [shards(): held = lax.all_to_all(chunks, AXIS, 0, 0, axis_index_groups=[order])]
    ppermute x1, starting transfers between devices: 0.13 us -> 0.55 us  [shards(): taken = lax.ppermute(given, AXIS, [(i, i ^ 1) for i in range(count)])]
where the time goes in v5:
time: 32.8 us; the launch traced here: 32.6 us
  waiting for transfers between devices  9.08 us (28%)
  starting transfers between devices  8.43 us (26%)
  blocking collectives  7.89 us (24%)
  Pallas kernels  7.01 us (21%)
    all_to_all x1, waiting for transfers between devices, shards(): held = lax.all_to_all(chunks, AXIS, 0, 0, axis_index_groups=[order])  9.08 us
    all_to_all x1, blocking collectives, shards(): sums = lax.all_to_all(sums, AXIS, 0, 0, axis_index_groups=[down])  7.89 us
    all_to_all x1, starting transfers between devices, shards(): held = lax.all_to_all(chunks, AXIS, 0, 0, axis_index_groups=[order])  7.88 us
    pallas_call x1, Pallas kernels, shards(): pl.pallas_call(grade_kernel, out_shape=(jax.ShapeDtypeStruct((count,) + c...  4.14 us
    pallas_call x1, Pallas kernels, shards(): pl.pallas_call(functools.partial(moment_kernel, columns), out_shape=(jax....  1.68 us
    pallas_call x1, Pallas kernels, shards(): pl.pallas_call(functools.partial(combine_kernel, columns), out_shape=jax....  1.19 us
  transfers between devices with their start and end apart: 2, of which 1 were waited for; matrix products, arithmetic and copies ran while one was open for 0% of the time, Pallas kernels for 0%

profile of v5, /device:TPU:0, one launch (start us, length us, event | category | flops | bytes accessed | tf_op | source)
XLA Modules:
  0.0 32.6 jit_solution(10127861475855641076)
XLA Ops:
  0.0 4.1 %grade.1 = (bf16[16,3,2,16,128]{4,3,2,1,0:T(8,128)(2,1)}, f32[4,8,128]{2,1,0:T(8,128)}) custom-call(f32[3,32]{1,0:T(4,128)} %bitcast.4, f32[32]{0:T(128)} %b_in_at.1, f32[3,32]{1,0:T(4,128)} %w_out_at.1, f32[3]{0:T(128)} %b_out_at.1, f32[3]{0:T(128)} %screen_at.1, bf16[1,3,32,960]{3,2,1,0:T(8,128)(2,1)} %video_at.1), custom_call_target="tpu_custom_call" | custom-call | tf_op jit(solution)/shard_map/grade/pallas_call | solution.py:351
  4.2 7.9 %all-to-all-start = ((bf16[16,3,2,16,128]{4,3,2,1,0:T(8,128)(2,1)}), bf16[16,3,2,16,128]{4,3,2,1,0:T(8,128)(2,1)S(1)}, u32[]{:S(2)}, u32[]{:S(2)}) async-start(bf16[16,3,2,16,128]{4,3,2,1,0:T(8,128)(2,1)} %get-tuple-element.11), calls=%async_computation | async-start | bytes 786432 | tf_op jit(solution)/shard_map/all_to_all | solution.py:375
  12.0 0.0 copy-start
  12.0 0.1 pad_maximum_fusion
  12.1 9.1 %all-to-all-done.held = bf16[16,3,2,16,128]{4,3,2,1,0:T(8,128)(2,1)S(1)} async-done(((bf16[16,3,2,16,128]{4,3,2,1,0:T(8,128)(2,1)}), bf16[16,3,2,16,128]{4,3,2,1,0:T(8,128)(2,1)S(1)}, u32[]{:S(2)}, u32[]{:S(2)}) %all-to-all-start) | async-done | bytes 393248 | tf_op jit(solution)/shard_map/all_to_all | solution.py:375
  21.2 0.1 broadcast_in_dim.2.place
  21.3 0.0 copy-done
  21.3 1.7 %moments.1 = (f32[16,1,128]{2,1,0:T(1,128)S(1)}, f32[3,3,16,8,128]{4,3,2,1,0:T(8,128)S(1)}, f32[3,3,16,8,128]{4,3,2,1,0:T(8,128)S(1)}, f32[8,128]{1,0:T(8,128)S(1)}) custom-call(f32[3,8,128]{2,1,0:T(8,128)S(1)} %broadcast_in_dim.2.place, bf16[16,3,2,16,128]{4,3,2,1,0:T(8,128)(2,1)S(1)} %all-to-all-done.held, f32[4,8,128]{2,1,0:T(8,128)S(1)} %copy-done), custom_call_target="tpu_custom_call" | custom-call | tf_op jit(solution)/shard_map/moments/pallas_call | solution.py:380
  22.9 0.6 %collective-permute-start = (f32[3,3,16,8,128]{4,3,2,1,0:T(8,128)S(1)}, f32[3,3,16,8,128]{4,3,2,1,0:T(8,128)S(1)}, u32[]{:S(2)}, u32[]{:S(2)}) collective-permute-start(f32[3,3,16,8,128]{4,3,2,1,0:T(8,128)S(1)} %get-tuple-element.16), channel_id=1, source_target_pairs={{0,1},{1,0},{2,3},{3,2},{4,5},{5,4},{6,7},{7,6},{8,9},{9,8},{10,11... | collective-permute-start | bytes 1769480 | tf_op jit(solution)/shard_map/ppermute | solution.py:393
  23.5 7.9 %all_to_all.10.sums = f32[16,1,128]{2,1,0:T(1,128)S(1)} all-to-all(f32[16,1,128]{2,1,0:T(1,128)S(1)} %get-tuple-element.14), channel_id=1, replica_groups={{15,14,13,12,11,10,9,8,7,6,5,4,3,2,1,0},{31,30,29,28,27,26,25,24,23,22,..., dimensions={0} | all-to-all | bytes 16384 | tf_op jit(solution)/shard_map/all_to_all | solution.py:395
  31.4 0.0 collective-permute-done.taken
  31.4 1.2 %combine.1 = f32[16,3,2,960]{3,2,1,0:T(2,128)} custom-call(f32[3,8,128]{2,1,0:T(8,128)S(1)} %broadcast_in_dim.2.place, f32[8,128]{1,0:T(8,128)S(1)} %get-tuple-element.13.sigma_at, f32[16,1,128]{2,1,0:T(1,128)S(1)} %all_to_all.10.sums, f32[3,3,16,8,128]{4,3,2,1,0:T(8,128)S(1)} %get-tuple-element.15.kept, f32[3,3,16,8,128]{4,3,2,1,0:T(8,128)S(1)} %collective-permute-done.taken), custom_call_target="tpu_custom_call" | custom-call | tf_op jit(solution)/shard_map/combine/pallas_call | solution.py:396
Async XLA Ops:
  4.2 17.0 %all-to-all-start = ((bf16[16,3,2,16,128]{4,3,2,1,0:T(8,128)(2,1)}), bf16[16,3,2,16,128]{4,3,2,1,0:T(8,128)(2,1)S(1)}, u32[]{:S(2)}, u32[]{:S(2)}) async-start(bf16[16,3,2,16,128]{4,3,2,1,0:T(8,128)(2,1)} %get-tuple-element.11), calls=%async_computation | async-start | bytes 786432 | tf_op jit(solution)/shard_map/all_to_all | solution.py:375
  12.0 9.2 %copy-start = (f32[4,8,128]{2,1,0:T(8,128)S(1)}, f32[4,8,128]{2,1,0:T(8,128)}, u32[]{:S(2)}) copy-start(f32[4,8,128]{2,1,0:T(8,128)} %get-tuple-element.12.extra) | copy-start | bytes 49156
  22.9 8.4 %collective-permute-start = (f32[3,3,16,8,128]{4,3,2,1,0:T(8,128)S(1)}, f32[3,3,16,8,128]{4,3,2,1,0:T(8,128)S(1)}, u32[]{:S(2)}, u32[]{:S(2)}) collective-permute-start(f32[3,3,16,8,128]{4,3,2,1,0:T(8,128)S(1)} %get-tuple-element.16), channel_id=1, source_target_pairs={{0,1},{1,0},{2,3},{3,2},{4,5},{5,4},{6,7},{7,6},{8,9},{9,8},{10,11... | collective-permute-start | bytes 1769480 | tf_op jit(solution)/shard_map/ppermute | solution.py:393

commit v6 on v5

--- a/solution.py
+++ b/solution.py
@@ -51,13 +51,12 @@
 
 
 def grade_kernel(
-    w_in_at, b_in_at, w_out_at, b_out_at, screen_at, video_at, chunks, extra,
-    w_in, b_in, w_out, b_out, screen, video, arrived, sent,
-    graded, tiles, first, second, ready, notes,
+    w_in_at, b_in_at, w_out_at, b_out_at, screen_at, video_at, chunks,
+    w_in, b_in, w_out, b_out, screen, video, arrived, sent, graded, first, second, ready,
 ):
     channels, rows, columns = video.shape[1:]
     units = b_in.shape[0]
-    across = graded.shape[2]
+    across = -(-columns // LANES) * LANES
     width = columns // BLOCKS
     halo = (LANES - width) // 2
     chips = chunks.shape[0] // 2
@@ -70,8 +69,13 @@
             ]
         )
     ]
-    pixels_in = pltpu.make_async_copy(video_at, video, arrived.at[5])
-    pixels_in.start()
+
+    def pixels_in(step):
+        part = (slice(None), slice(None), pl.ds(pl.multiple_of(step * 16, 16), 16))
+        return pltpu.make_async_copy(video_at.at[part], video.at[part], arrived.at[5 + step])
+
+    for step in range(rows // 16):
+        pixels_in(step).start()
     for copy in weights:
         copy.start()
     for copy in weights:
@@ -98,27 +102,41 @@
         mix[c][c] = mix[c][c] + 1.0
         mix[c][channels] = mix[c][channels] + b_out[c]
     layer = first[...].astype(jnp.bfloat16)
-    pixels_in.wait()
-
-    span = across // 2
-    times = span // LANES
+
+    half_blocks = BLOCKS // 2
+    span = half_blocks * LANES
+    zero = jnp.zeros(TILE, jnp.float32)
+    upper = sublane % 2 == 0
+    masks = []
+    for side in range(2):
+        column = (sublane // 2 + side * half_blocks) * width - halo + lane
+        masks.append((column >= 0) & (column < columns))
 
     def wide(tile):
-        return jnp.tile(tile, (1, times))
+        return jnp.tile(tile, (1, half_blocks))
+
+    def cut(band):
+        parts = []
+        for s in range(BLOCKS):
+            start = s * width - halo
+            v, off = start // LANES, start % LANES
+            low = band[:, v * LANES : (v + 1) * LANES] if v >= 0 else zero
+            high = band[:, (v + 1) * LANES : (v + 2) * LANES]
+            parts.append(pltpu.roll(jnp.where(lane >= off, low, high), LANES - off, 1))
+        return turn_pairs(parts[:half_blocks]), turn_pairs(parts[half_blocks:])
 
     def grade(step, _):
+        pixels_in(step).wait()
         top = pl.multiple_of(step * 16, 16)
-        for start in range(0, across, span):
-            count = min(span, columns - start)
-            taken = []
-            for c in range(channels):
-                values = video[0, c, pl.ds(top, 16), start : start + count].astype(jnp.float32)
-                if count < span:
-                    empty = jnp.zeros((16, span - count), jnp.float32)
-                    values = jnp.concatenate([values, empty], axis=1)
-                taken.append(values)
-            for r in (0, 8):
-                pixels = [values[r : r + 8] for values in taken]
+        taken = []
+        for c in range(channels):
+            values = video[0, c, pl.ds(top, 16), :].astype(jnp.float32)
+            empty = jnp.zeros((16, across - columns), jnp.float32)
+            taken.append(jnp.concatenate([values, empty], axis=1))
+        for r in (0, 8):
+            sides = [cut(values[r : r + 8]) for values in taken]
+            for side in range(2):
+                pixels = [jnp.concatenate(sides[c][side], axis=1) for c in range(channels)]
                 group = jnp.concatenate(pixels + [jnp.ones((8, span), jnp.float32)], axis=0)
                 group = group.astype(jnp.bfloat16)
                 group = jnp.concatenate([group] * 3 + [jnp.zeros_like(group)], axis=0)
@@ -134,62 +152,59 @@
                     unit = h * jnp.tanh(h)
                     for c in range(channels):
                         total[c] = total[c] + wide(second[c, j]) * unit
-                inside = start + lanes_of((8, span)) < columns
                 for c in range(channels):
-                    graded[c, pl.ds(top + r, 8), start : start + span] = jnp.where(
-                        inside, total[c], 0.0
-                    )
+                    for k in range(half_blocks):
+                        tile = total[c][:, k * LANES : (k + 1) * LANES]
+                        at = step * 8 + r // 2 + k
+                        graded[c, side, at] = jnp.where(masks[side], tile, 0.0)
         return 0
 
-    lax.fori_loop(0, rows // 16, grade, 0)
-
-    line = sublanes_of((rows, across))
-    inside = lanes_of((rows, across)) < columns
-    upper = sublane % 2 == 0
-    zero = jnp.zeros(TILE, jnp.float32)
-    sigma = jnp.full(TILE, 1.0, jnp.float32)
+    lax.fori_loop(0, rows // 16, grade, 0, unroll=2)
+
+    pairs = rows // 2
     copies = []
     for c in range(channels):
-        sigma = jnp.where(lane == c, 6.0 + screen[c], sigma)
-        g = graded[c]
-        above = jnp.where(line == 0, 0.0, pltpu.roll(g, 1, 0))
-        below = jnp.where(line == rows - 1, 0.0, pltpu.roll(g, rows - 1, 0))
-        beside = pltpu.roll(g, 1, 1) + pltpu.roll(g, across - 1, 1)
-        target = (screen[c] + 4.0) * g - (above + below + beside)
-        target = jnp.where(inside, target, 0.0).astype(jnp.bfloat16).astype(jnp.float32)
-        for top in range(0, rows, 8):
-            band = target[top : top + 8]
-            parts = []
-            for s in range(BLOCKS):
-                start = s * width - halo
-                v, off = start // LANES, start % LANES
-                low = zero
-                if v >= 0:
-                    low = pltpu.roll(band[:, v * LANES : (v + 1) * LANES], (LANES - off) % LANES, 1)
-                high = pltpu.roll(band[:, (v + 1) * LANES : (v + 2) * LANES], LANES - off, 1)
-                parts.append(jnp.where(lane < LANES - off, low, high))
-            for side in range(2):
-                for k, tile in enumerate(turn_pairs(parts[4 * side : 4 * side + 4])):
-                    tiles[c, side, top // 2 + k] = tile
-        pairs = rows // 2
         for side in range(2):
-
-            def pair(k):
-                return tiles[c, side, k] if 0 <= k < pairs else zero
-
+            field = [graded[c, side, k] for k in range(pairs)]
+            between = [
+                field[0], *[field[k] + field[k + 1] for k in range(pairs - 1)], field[pairs - 1]
+            ]
+            target = [zero]
+            for k in range(pairs):
+                beyond = jnp.where(
+                    upper, pltpu.roll(between[k], 7, 0), pltpu.roll(between[k + 1], 1, 0)
+                )
+                beyond = beyond + (pltpu.roll(field[k], 1, 1) + pltpu.roll(field[k], LANES - 1, 1))
+                value = (screen[c] + 4.0) * field[k] - beyond
+                target.append(jnp.where(masks[side], value, 0.0))
+            target.append(zero)
             for q in range(chips):
+                at = (first_member(2 * chips) - (2 * q + side)) % (2 * chips)
                 for p in range(2):
-                    k = 2 * q - 1 + 2 * p
-                    both = jnp.concatenate([pair(k), pair(k + 1)], axis=0)
-                    at = (first_member(2 * chips) - (2 * q + side)) % (2 * chips)
+                    k = 2 * q + 2 * p
+                    both = jnp.concatenate([target[k], target[k + 1]], axis=0)
                     ready[c, at, p] = both.astype(jnp.bfloat16)
         copies.append(pltpu.make_async_copy(ready.at[c], chunks.at[:, c], sent.at[c]))
         copies[-1].start()
-
+    for copy in copies:
+        copy.wait()
+
+
+def fifth_kernel(screen, chunks, extra):
+    chips, channels = chunks.shape[0] // 2, chunks.shape[1]
+    upper = sublanes_of(TILE) % 2 == 0
+    zero = jnp.zeros(TILE, jnp.float32)
+    sigma = jnp.full(TILE, 1.0, jnp.float32)
+    pairs = 2 * chips
     for c in range(channels):
+        sigma = jnp.where(lanes_of(TILE) == c, 6.0 + screen[c], sigma)
         total = zero
         for side in range(2):
-            field = [tiles[c, side, k] for k in range(pairs)]
+            field = []
+            for q in range(chips):
+                at = (first_member(2 * chips) - (2 * q + side)) % (2 * chips)
+                field.append(chunks[at, c, 0].astype(jnp.float32)[8:])
+                field.append(chunks[at, c, 1].astype(jnp.float32)[:8])
             twice = []
             for k in range(pairs):
                 beyond = zero
@@ -206,12 +221,8 @@
             for k in range(pairs):
                 after = pltpu.roll(twice[k + 1], 1, 0) if k < pairs - 1 else zero
                 total = total + twice[k] * jnp.where(upper, pltpu.roll(twice[k], 7, 0), after)
-        notes[c] = total + total
-    notes[channels] = sigma
-    copies.append(pltpu.make_async_copy(notes, extra, sent.at[channels]))
-    copies[-1].start()
-    for copy in copies:
-        copy.wait()
+        extra[c] = total + total
+    extra[channels] = sigma
 
 
 def within(field, mask):
@@ -219,6 +230,15 @@
     frames = jnp.concatenate([field[1:], zero], axis=0) + jnp.concatenate([zero, field[:-1]], axis=0)
     beside = pltpu.roll(field, 1, 2) + pltpu.roll(field, LANES - 1, 2)
     return frames + jnp.where(mask, beside, 0.0)
+
+
+def half_form(field):
+    zero = jnp.zeros_like(field[:1])
+    return field * (jnp.concatenate([zero, field[:-1]], axis=0) + pltpu.roll(field, 1, 2))
+
+
+GAMMA = (5.0 - 5.0**0.5) / 4.0
+DELTA = (5.0 + 5.0**0.5) / 10.0
 
 
 def moment_kernel(columns, place, held, extra, sums, kept, given, sigma):
@@ -253,10 +273,11 @@
             u2 = b[i - 1] + (top if i == 1 else bottom) * u0 + b[i + 1]
             k0 = within(u0, mask)
             k1 = within(u1, mask)
-            y = 2.0 * k1 + within(k0, mask)
-            y1 = 2.0 * within(u2, mask) + within(k1, mask)
+            kk0 = within(k0, mask)
             n1 = u1 + k0
-            n2 = u2 + y
+            n2 = u2 + 2.0 * k1 + kk0
+            z = kk0 + 2.5 * k1 + GAMMA * u2
+            t = u2 + DELTA * k1
             sides.append((u0, n1, n2))
             products = [
                 u0 * u0,
@@ -264,7 +285,7 @@
                 n1 * n1,
                 n1 * n2,
                 n2 * n2,
-                n2 * within(n2, mask) + y * y1 + 2.0 * (y1 * u2),
+                2.0 * half_form(z) + (2.0 * (5.0 - GAMMA * GAMMA)) * half_form(t),
             ]
             for k, product in enumerate(products):
                 totals[k] = totals[k] + jnp.sum(product, axis=0)
@@ -345,31 +366,34 @@
     _, channels, rows, columns = video.shape
     units = b_in.shape[0]
     frames = count
-    across = -(-columns // LANES) * LANES
     operands = (w_in.T, b_in, w_out, b_out, screen, video)
     chunk = (channels, 2, 16, LANES)
-    chunks, extra = pl.pallas_call(
+    chunks = pl.pallas_call(
         grade_kernel,
-        out_shape=(
-            jax.ShapeDtypeStruct((count,) + chunk, jnp.bfloat16),
-            jax.ShapeDtypeStruct((channels + 1,) + TILE, jnp.float32),
-        ),
+        out_shape=jax.ShapeDtypeStruct((count,) + chunk, jnp.bfloat16),
         in_specs=[hbm()] * 6,
-        out_specs=(hbm(),) * 2,
+        out_specs=hbm(),
         scratch_shapes=[pltpu.SMEM(a.shape, a.dtype) for a in operands[:-1]]
         + [
             pltpu.VMEM(video.shape, video.dtype),
-            pltpu.SemaphoreType.DMA((6,)),
-            pltpu.SemaphoreType.DMA((channels + 1,)),
-            pltpu.VMEM((channels, rows, across), jnp.float32),
+            pltpu.SemaphoreType.DMA((5 + rows // 16,)),
+            pltpu.SemaphoreType.DMA((channels,)),
             pltpu.VMEM((channels, 2, rows // 2) + TILE, jnp.float32),
             pltpu.VMEM((8 * units, LANES), jnp.float32),
             pltpu.VMEM((channels, units) + TILE, jnp.float32),
             pltpu.VMEM((channels, count) + chunk[1:], jnp.bfloat16),
-            pltpu.VMEM((channels + 1,) + TILE, jnp.float32),
         ],
         name="grade",
     )(*operands)
+    extra = pl.pallas_call(
+        fifth_kernel,
+        out_shape=jax.ShapeDtypeStruct((channels + 1,) + TILE, jnp.float32),
+        in_specs=[pl.BlockSpec(memory_space=pltpu.SMEM), vmem()],
+        out_specs=vmem(),
+        compiler_params=params(),
+        cost_estimate=pl.CostEstimate(flops=1 << 20, bytes_accessed=1 << 20, transcendentals=0),
+        name="fifth",
+    )(screen, chunks)
     first = first_member(count)
     order = [(first - i) % count for i in range(count)]
     held = lax.all_to_all(chunks, AXIS, 0, 0, axis_index_groups=[order])

time: 32.8 us -> 32.6 us (level)
  waiting for transfers between devices: 9.08 us -> 7.77 us
  local copies, waits for them, and re-layouts: 0.07 us -> 0.71 us
    all_to_all x1, waiting for transfers between devices: 9.08 us -> 7.77 us  [shards(): held = lax.all_to_all(chunks, AXIS, 0, 0, axis_index_groups=[order])]
    unnamed x2 -> x4, local copies, waits for them, and re-layouts: 0.01 us -> 0.64 us
    pallas_call x1 -> x2, Pallas kernels: 4.14 us -> 4.56 us  [the longest x1 3.9 us: shards(): pl.pallas_call(grade_kernel, out_shape=jax.ShapeDtypeStruct((count,) + ch...]
  transfers between devices with their start and end apart: 2 -> 2, of which waited for: 1 -> 1; matrix products, arithmetic and copies ran while one was open for 0% -> 0% of each run, Pallas kernels for 0% -> 2%
where the time goes in v6:
time: 32.6 us; the launch traced here: 32.3 us
  starting transfers between devices  8.55 us (26%)
  blocking collectives  7.89 us (24%)
  waiting for transfers between devices  7.77 us (24%)
  Pallas kernels  7.24 us (22%)
  local copies, waits for them, and re-layouts  0.71 us (2%)
    all_to_all x1, starting transfers between devices, shards(): held = lax.all_to_all(chunks, AXIS, 0, 0, axis_index_groups=[order])  8.01 us
    all_to_all x1, blocking collectives, shards(): sums = lax.all_to_all(sums, AXIS, 0, 0, axis_index_groups=[down])  7.89 us
    all_to_all x1, waiting for transfers between devices, shards(): held = lax.all_to_all(chunks, AXIS, 0, 0, axis_index_groups=[order])  7.77 us
    pallas_call x1, Pallas kernels, shards(): pl.pallas_call(grade_kernel, out_shape=jax.ShapeDtypeStruct((count,) + ch...  3.9 us
    pallas_call x1, Pallas kernels, shards(): pl.pallas_call(functools.partial(moment_kernel, columns), out_shape=(jax....  1.51 us
    pallas_call x1, Pallas kernels, shards(): pl.pallas_call(functools.partial(combine_kernel, columns), out_shape=jax....  1.17 us
    pallas_call x1, Pallas kernels, shards(): pl.pallas_call(fifth_kernel, out_shape=jax.ShapeDtypeStruct((channels + 1...  0.66 us
  transfers between devices with their start and end apart: 2, of which 1 were waited for; matrix products, arithmetic and copies ran while one was open for 0% of the time, Pallas kernels for 2%

profile of v6, /device:TPU:0, one launch (start us, length us, event | category | flops | bytes accessed | tf_op | source)
XLA Modules:
  0.0 32.3 jit_solution(6323811962065020865)
XLA Ops:
  0.0 3.9 %grade.1.chunks = bf16[16,3,2,16,128]{4,3,2,1,0:T(8,128)(2,1)} custom-call(f32[3,32]{1,0:T(4,128)} %bitcast.4, f32[32]{0:T(128)} %b_in_at.1, f32[3,32]{1,0:T(4,128)} %w_out_at.1, f32[3]{0:T(128)} %b_out_at.1, f32[3]{0:T(128)} %screen.1, bf16[1,3,32,960]{3,2,1,0:T(8,128)(2,1)} %video_at.1), custom_call_target="tpu_custom_call" | custom-call | tf_op jit(solution)/shard_map/grade/pallas_call | solution.py:371
  3.9 0.0 copy-start
  3.9 8.0 %all-to-all-start = ((bf16[16,3,2,16,128]{4,3,2,1,0:T(8,128)(2,1)}), bf16[16,3,2,16,128]{4,3,2,1,0:T(8,128)(2,1)S(1)}, u32[]{:S(2)}, u32[]{:S(2)}) async-start(bf16[16,3,2,16,128]{4,3,2,1,0:T(8,128)(2,1)} %grade.1.chunks), calls=%async_computation | async-start | bytes 786432 | tf_op jit(solution)/shard_map/all_to_all | solution.py:399
  11.9 0.0 copy-start.1
  11.9 0.0 copy-done
  12.0 0.6 %copy-done.1 = f32[3]{0:T(128)S(1)} copy-done((f32[3]{0:T(128)S(1)}, f32[3]{0:T(128)}, u32[]{:S(2)}) %copy-start.1) | copy-done | bytes 36
  12.6 0.7 %fifth.1.extra = f32[4,8,128]{2,1,0:T(8,128)S(1)} custom-call(f32[3]{0:T(128)S(1)} %copy-done.1, bf16[16,3,2,16,128]{4,3,2,1,0:T(8,128)(2,1)S(1)} %copy-done), custom_call_target="tpu_custom_call" | custom-call | flops 1048576 | bytes 1048576 | tf_op jit(solution)/shard_map/fifth/pallas_call | solution.py:388
  13.3 0.1 pad_maximum_fusion
  13.3 7.8 %all-to-all-done.held = bf16[16,3,2,16,128]{4,3,2,1,0:T(8,128)(2,1)S(1)} async-done(((bf16[16,3,2,16,128]{4,3,2,1,0:T(8,128)(2,1)}), bf16[16,3,2,16,128]{4,3,2,1,0:T(8,128)(2,1)S(1)}, u32[]{:S(2)}, u32[]{:S(2)}) %all-to-all-start) | async-done | bytes 393248 | tf_op jit(solution)/shard_map/all_to_all | solution.py:399
  21.1 0.1 broadcast_in_dim.2.place
  21.2 1.5 %moments.1 = (f32[16,1,128]{2,1,0:T(1,128)S(1)}, f32[3,3,16,8,128]{4,3,2,1,0:T(8,128)S(1)}, f32[3,3,16,8,128]{4,3,2,1,0:T(8,128)S(1)}, f32[8,128]{1,0:T(8,128)S(1)}) custom-call(f32[3,8,128]{2,1,0:T(8,128)S(1)} %broadcast_in_dim.2.place, bf16[16,3,2,16,128]{4,3,2,1,0:T(8,128)(2,1)S(1)} %all-to-all-done.held, f32[4,8,128]{2,1,0:T(8,128)S(1)} %fifth.1.extra), custom_call_target="tpu_custom_call" | custom-call | tf_op jit(solution)/shard_map/moments/pallas_call | solution.py:404
  22.7 0.5 %collective-permute-start = (f32[3,3,16,8,128]{4,3,2,1,0:T(8,128)S(1)}, f32[3,3,16,8,128]{4,3,2,1,0:T(8,128)S(1)}, u32[]{:S(2)}, u32[]{:S(2)}) collective-permute-start(f32[3,3,16,8,128]{4,3,2,1,0:T(8,128)S(1)} %get-tuple-element.12), channel_id=1, source_target_pairs={{0,1},{1,0},{2,3},{3,2},{4,5},{5,4},{6,7},{7,6},{8,9},{9,8},{10,11... | collective-permute-start | bytes 1769480 | tf_op jit(solution)/shard_map/ppermute | solution.py:417
  23.2 7.9 %all_to_all.10.sums = f32[16,1,128]{2,1,0:T(1,128)S(1)} all-to-all(f32[16,1,128]{2,1,0:T(1,128)S(1)} %get-tuple-element.10), channel_id=1, replica_groups={{15,14,13,12,11,10,9,8,7,6,5,4,3,2,1,0},{31,30,29,28,27,26,25,24,23,22,..., dimensions={0} | all-to-all | bytes 16384 | tf_op jit(solution)/shard_map/all_to_all | solution.py:419
  31.1 0.0 collective-permute-done.taken
  31.1 1.2 %combine.1 = f32[16,3,2,960]{3,2,1,0:T(2,128)} custom-call(f32[3,8,128]{2,1,0:T(8,128)S(1)} %broadcast_in_dim.2.place, f32[8,128]{1,0:T(8,128)S(1)} %get-tuple-element.9.sigma_at, f32[16,1,128]{2,1,0:T(1,128)S(1)} %all_to_all.10.sums, f32[3,3,16,8,128]{4,3,2,1,0:T(8,128)S(1)} %get-tuple-element.11.kept, f32[3,3,16,8,128]{4,3,2,1,0:T(8,128)S(1)} %collective-permute-done.taken), custom_call_target="tpu_custom_call" | custom-call | tf_op jit(solution)/shard_map/combine/pallas_call | solution.py:420
Async XLA Ops:
  3.9 8.0 %copy-start = (bf16[16,3,2,16,128]{4,3,2,1,0:T(8,128)(2,1)S(1)}, bf16[16,3,2,16,128]{4,3,2,1,0:T(8,128)(2,1)}, u32[]{:S(2)}) copy-start(bf16[16,3,2,16,128]{4,3,2,1,0:T(8,128)(2,1)} %grade.1.chunks) | copy-start | bytes 1179652
  3.9 17.2 %all-to-all-start = ((bf16[16,3,2,16,128]{4,3,2,1,0:T(8,128)(2,1)}), bf16[16,3,2,16,128]{4,3,2,1,0:T(8,128)(2,1)S(1)}, u32[]{:S(2)}, u32[]{:S(2)}) async-start(bf16[16,3,2,16,128]{4,3,2,1,0:T(8,128)(2,1)} %grade.1.chunks), calls=%async_computation | async-start | bytes 786432 | tf_op jit(solution)/shard_map/all_to_all | solution.py:399
  11.9 0.7 %copy-start.1 = (f32[3]{0:T(128)S(1)}, f32[3]{0:T(128)}, u32[]{:S(2)}) copy-start(f32[3]{0:T(128)} %screen.1) | copy-start | bytes 40
  22.7 8.4 %collective-permute-start = (f32[3,3,16,8,128]{4,3,2,1,0:T(8,128)S(1)}, f32[3,3,16,8,128]{4,3,2,1,0:T(8,128)S(1)}, u32[]{:S(2)}, u32[]{:S(2)}) collective-permute-start(f32[3,3,16,8,128]{4,3,2,1,0:T(8,128)S(1)} %get-tuple-element.12), channel_id=1, source_target_pairs={{0,1},{1,0},{2,3},{3,2},{4,5},{5,4},{6,7},{7,6},{8,9},{9,8},{10,11... | collective-permute-start | bytes 1769480 | tf_op jit(solution)/shard_map/ppermute | solution.py:417

commit v7 on v6

--- a/solution.py
+++ b/solution.py
@@ -225,11 +225,25 @@
     extra[channels] = sigma
 
 
-def within(field, mask):
+def frames_of(field):
     zero = jnp.zeros_like(field[:1])
-    frames = jnp.concatenate([field[1:], zero], axis=0) + jnp.concatenate([zero, field[:-1]], axis=0)
-    beside = pltpu.roll(field, 1, 2) + pltpu.roll(field, LANES - 1, 2)
-    return frames + jnp.where(mask, beside, 0.0)
+    return jnp.concatenate([field[1:], zero], axis=0) + jnp.concatenate([zero, field[:-1]], axis=0)
+
+
+def rows_of(before, after):
+    upper = (sublanes_of(TILE) % 2 == 0)[None]
+    return jnp.where(upper, pltpu.roll(before, 7, 1), pltpu.roll(after, 1, 1))
+
+
+def bands(low, high):
+    shape = (LANES, LANES)
+    i, j = sublanes_of(shape), lanes_of(shape)
+    gap = jnp.abs(i - j)
+    inside = (i >= low) & (i < high) & (j >= low) & (j < high)
+    once = jnp.where(inside & (gap == 1), 1.0, 0.0)
+    ends = jnp.where(i == low, 1.0, 0.0) + jnp.where(i == high - 1, 1.0, 0.0)
+    twice = jnp.where(gap == 0, 2.0 - ends, jnp.where(gap == 2, 1.0, 0.0))
+    return once, jnp.where(inside, twice, 0.0)
 
 
 def half_form(field):
@@ -247,33 +261,49 @@
     halo = (LANES - width) // 2
     odd = place[2] > 0.5
     lane, sublane = lanes_of(TILE), sublanes_of(TILE)
-    block = sublane // 2 + jnp.where(odd, BLOCKS // 2, 0)
-    column = block * width - halo + lane
-    mask = ((column >= 0) & (column < columns))[None]
     own = (lane >= halo) & (lane < halo + width)
     upper = (sublane % 2 == 0)[None]
     top = jnp.where(upper, place[0][None], 2.0)
     bottom = jnp.where(upper, 2.0, place[1][None])
-    out_lane = lanes_of((1, LANES))
-    result = jnp.zeros((1, LANES), jnp.float32)
+    side = jnp.max(place[2])
+    first_lane = jnp.where(side > 0.5, 0, halo)
+    last_lane = jnp.where(side > 0.5, halo + width, LANES)
+    matrix = jnp.concatenate([*bands(0, LANES), *bands(first_lane, last_lane)], axis=1)
+    matrix = matrix.astype(jnp.bfloat16)
+    rows = sublanes_of((2 * TILE[0], LANES)) % TILE[0] // 2
+    edge = (rows == jnp.where(side > 0.5, BLOCKS // 2 - 1, 0))[None]
+    result = jnp.zeros(TILE, jnp.float32)
+    turn = first_member(frames) + 1
     for c in range(channels):
-        turn = first_member(frames) + 1
-        halves = [
-            jnp.concatenate([held[turn:, c, p], held[:turn, c, p]], axis=0).astype(jnp.float32)
-            for p in range(2)
-        ]
-        b = [halves[0][:, :8], halves[0][:, 8:], halves[1][:, :8], halves[1][:, 8:]]
-        between = [b[i] + b[i + 1] for i in range(3)]
+        b, g, h = [], [], []
+        for p in range(2):
+            both = jnp.concatenate([held[turn:, c, p], held[:turn, c, p]], axis=0)
+            columned = jnp.dot(
+                both.reshape(frames * 2 * TILE[0], LANES),
+                matrix,
+                preferred_element_type=jnp.float32,
+            ).reshape(frames, 2 * TILE[0], 4 * LANES)
+            plain, twice, cut, cut_twice = (
+                columned[:, :, k * LANES : (k + 1) * LANES] for k in range(4)
+            )
+            for into, values in (
+                (b, both.astype(jnp.float32)),
+                (g, jnp.where(edge, cut, plain)),
+                (h, jnp.where(edge, cut_twice, twice)),
+            ):
+                into += [values[:, : TILE[0]], values[:, TILE[0] :]]
+        b_sums = [b[i] + b[i + 1] for i in range(3)]
+        g_sums = [g[i] + g[i + 1] for i in range(3)]
         totals = [jnp.zeros(TILE, jnp.float32) for _ in range(6)]
         totals[5] = extra[c]
         sides = []
         for i in (1, 2):
             u0 = b[i]
-            u1 = jnp.where(upper, pltpu.roll(between[i - 1], 7, 1), pltpu.roll(between[i], 1, 1))
+            u1 = rows_of(b_sums[i - 1], b_sums[i])
             u2 = b[i - 1] + (top if i == 1 else bottom) * u0 + b[i + 1]
-            k0 = within(u0, mask)
-            k1 = within(u1, mask)
-            kk0 = within(k0, mask)
+            k0 = frames_of(u0) + g[i]
+            k1 = frames_of(u1) + rows_of(g_sums[i - 1], g_sums[i])
+            kk0 = frames_of(k0 + g[i]) + h[i]
             n1 = u1 + k0
             n2 = u2 + 2.0 * k1 + kk0
             z = kk0 + 2.5 * k1 + GAMMA * u2
@@ -292,11 +322,13 @@
         for k in range(3):
             kept[k, c] = jnp.where(odd[None], sides[1][k], sides[0][k])
             given[k, c] = jnp.where(odd[None], sides[0][k], sides[1][k])
+        lines = jnp.zeros(TILE, jnp.float32)
         for k, total in enumerate(totals):
-            total = jnp.where(own, total, 0.0)
-            total = jnp.sum(total, axis=0, keepdims=True)
-            total = jnp.sum(total, axis=1, keepdims=True)
-            result = jnp.where(out_lane == 8 * k + c, total, result)
+            total = jnp.sum(jnp.where(own, total, 0.0), axis=0, keepdims=True)
+            lines = jnp.where(sublane == k, total, lines)
+        column = jnp.sum(lines, axis=1, keepdims=True)
+        result = jnp.where(lane == 8 * sublane + c, column, result)
+    result = jnp.sum(result, axis=0, keepdims=True)
     sums[...] = jnp.broadcast_to(result[None], sums.shape)
     sigma[...] = extra[channels]
 

time: 32.6 us -> 32.3 us (level)
  Pallas kernels: 7.24 us -> 6.89 us
    pallas_call x1, Pallas kernels: 1.51 us -> 1.15 us  [shards(): pl.pallas_call(functools.partial(moment_kernel, columns), out_shape=(jax....]
where the time goes in v7:
time: 32.3 us; the launch traced here: 32 us
  starting transfers between devices  8.59 us (27%)
  blocking collectives  7.89 us (24%)
  waiting for transfers between devices  7.77 us (24%)
  Pallas kernels  6.89 us (21%)
  local copies, waits for them, and re-layouts  0.71 us (2%)
    all_to_all x1, starting transfers between devices, shards(): held = lax.all_to_all(chunks, AXIS, 0, 0, axis_index_groups=[order])  8.01 us
    all_to_all x1, blocking collectives, shards(): sums = lax.all_to_all(sums, AXIS, 0, 0, axis_index_groups=[down])  7.89 us
    all_to_all x1, waiting for transfers between devices, shards(): held = lax.all_to_all(chunks, AXIS, 0, 0, axis_index_groups=[order])  7.77 us
    pallas_call x1, Pallas kernels, shards(): pl.pallas_call(grade_kernel, out_shape=jax.ShapeDtypeStruct((count,) + ch...  3.9 us
    pallas_call x1, Pallas kernels, shards(): pl.pallas_call(functools.partial(combine_kernel, columns), out_shape=jax....  1.17 us
    pallas_call x1, Pallas kernels, shards(): pl.pallas_call(functools.partial(moment_kernel, columns), out_shape=(jax....  1.15 us
    pallas_call x1, Pallas kernels, shards(): pl.pallas_call(fifth_kernel, out_shape=jax.ShapeDtypeStruct((channels + 1...  0.66 us
  transfers between devices with their start and end apart: 2, of which 1 were waited for; matrix products, arithmetic and copies ran while one was open for 0% of the time, Pallas kernels for 2%

profile of v7, /device:TPU:0, one launch (start us, length us, event | category | flops | bytes accessed | tf_op | source)
XLA Modules:
  0.0 32.0 jit_solution(11797287388980675186)
XLA Ops:
  0.0 3.9 %grade.1.chunks = bf16[16,3,2,16,128]{4,3,2,1,0:T(8,128)(2,1)} custom-call(f32[3,32]{1,0:T(4,128)} %bitcast.4, f32[32]{0:T(128)} %b_in_at.1, f32[3,32]{1,0:T(4,128)} %w_out_at.1, f32[3]{0:T(128)} %b_out_at.1, f32[3]{0:T(128)} %screen.1, bf16[1,3,32,960]{3,2,1,0:T(8,128)(2,1)} %video_at.1), custom_call_target="tpu_custom_call" | custom-call | tf_op jit(solution)/shard_map/grade/pallas_call | solution.py:403
  3.9 0.0 copy-start
  3.9 8.0 %all-to-all-start = ((bf16[16,3,2,16,128]{4,3,2,1,0:T(8,128)(2,1)}), bf16[16,3,2,16,128]{4,3,2,1,0:T(8,128)(2,1)S(1)}, u32[]{:S(2)}, u32[]{:S(2)}) async-start(bf16[16,3,2,16,128]{4,3,2,1,0:T(8,128)(2,1)} %grade.1.chunks), calls=%async_computation | async-start | bytes 786432 | tf_op jit(solution)/shard_map/all_to_all | solution.py:431
  11.9 0.0 copy-start.1
  11.9 0.0 copy-done
  12.0 0.6 %copy-done.1 = f32[3]{0:T(128)S(1)} copy-done((f32[3]{0:T(128)S(1)}, f32[3]{0:T(128)}, u32[]{:S(2)}) %copy-start.1) | copy-done | bytes 36
  12.6 0.7 %fifth.1.extra = f32[4,8,128]{2,1,0:T(8,128)S(1)} custom-call(f32[3]{0:T(128)S(1)} %copy-done.1, bf16[16,3,2,16,128]{4,3,2,1,0:T(8,128)(2,1)S(1)} %copy-done), custom_call_target="tpu_custom_call" | custom-call | flops 1048576 | bytes 1048576 | tf_op jit(solution)/shard_map/fifth/pallas_call | solution.py:420
  13.3 0.1 pad_maximum_fusion
  13.3 7.8 %all-to-all-done.held = bf16[16,3,2,16,128]{4,3,2,1,0:T(8,128)(2,1)S(1)} async-done(((bf16[16,3,2,16,128]{4,3,2,1,0:T(8,128)(2,1)}), bf16[16,3,2,16,128]{4,3,2,1,0:T(8,128)(2,1)S(1)}, u32[]{:S(2)}, u32[]{:S(2)}) %all-to-all-start) | async-done | bytes 393248 | tf_op jit(solution)/shard_map/all_to_all | solution.py:431
  21.1 0.1 broadcast_in_dim.2.place
  21.2 1.2 %moments.1 = (f32[16,1,128]{2,1,0:T(1,128)S(1)}, f32[3,3,16,8,128]{4,3,2,1,0:T(8,128)S(1)}, f32[3,3,16,8,128]{4,3,2,1,0:T(8,128)S(1)}, f32[8,128]{1,0:T(8,128)S(1)}) custom-call(f32[3,8,128]{2,1,0:T(8,128)S(1)} %broadcast_in_dim.2.place, bf16[16,3,2,16,128]{4,3,2,1,0:T(8,128)(2,1)S(1)} %all-to-all-done.held, f32[4,8,128]{2,1,0:T(8,128)S(1)} %fifth.1.extra), custom_call_target="tpu_custom_call" | custom-call | tf_op jit(solution)/shard_map/moments/pallas_call | solution.py:436
  22.3 0.6 %collective-permute-start = (f32[3,3,16,8,128]{4,3,2,1,0:T(8,128)S(1)}, f32[3,3,16,8,128]{4,3,2,1,0:T(8,128)S(1)}, u32[]{:S(2)}, u32[]{:S(2)}) collective-permute-start(f32[3,3,16,8,128]{4,3,2,1,0:T(8,128)S(1)} %get-tuple-element.12), channel_id=1, source_target_pairs={{0,1},{1,0},{2,3},{3,2},{4,5},{5,4},{6,7},{7,6},{8,9},{9,8},{10,11... | collective-permute-start | bytes 1769480 | tf_op jit(solution)/shard_map/ppermute | solution.py:449
  22.9 7.9 %all_to_all.10.sums = f32[16,1,128]{2,1,0:T(1,128)S(1)} all-to-all(f32[16,1,128]{2,1,0:T(1,128)S(1)} %get-tuple-element.10), channel_id=1, replica_groups={{15,14,13,12,11,10,9,8,7,6,5,4,3,2,1,0},{31,30,29,28,27,26,25,24,23,22,..., dimensions={0} | all-to-all | bytes 16384 | tf_op jit(solution)/shard_map/all_to_all | solution.py:451
  30.8 0.0 collective-permute-done.taken
  30.8 1.2 %combine.1 = f32[16,3,2,960]{3,2,1,0:T(2,128)} custom-call(f32[3,8,128]{2,1,0:T(8,128)S(1)} %broadcast_in_dim.2.place, f32[8,128]{1,0:T(8,128)S(1)} %get-tuple-element.9.sigma_at, f32[16,1,128]{2,1,0:T(1,128)S(1)} %all_to_all.10.sums, f32[3,3,16,8,128]{4,3,2,1,0:T(8,128)S(1)} %get-tuple-element.11.kept, f32[3,3,16,8,128]{4,3,2,1,0:T(8,128)S(1)} %collective-permute-done.taken), custom_call_target="tpu_custom_call" | custom-call | tf_op jit(solution)/shard_map/combine/pallas_call | solution.py:452
Async XLA Ops:
  3.9 8.0 %copy-start = (bf16[16,3,2,16,128]{4,3,2,1,0:T(8,128)(2,1)S(1)}, bf16[16,3,2,16,128]{4,3,2,1,0:T(8,128)(2,1)}, u32[]{:S(2)}) copy-start(bf16[16,3,2,16,128]{4,3,2,1,0:T(8,128)(2,1)} %grade.1.chunks) | copy-start | bytes 1179652
  3.9 17.2 %all-to-all-start = ((bf16[16,3,2,16,128]{4,3,2,1,0:T(8,128)(2,1)}), bf16[16,3,2,16,128]{4,3,2,1,0:T(8,128)(2,1)S(1)}, u32[]{:S(2)}, u32[]{:S(2)}) async-start(bf16[16,3,2,16,128]{4,3,2,1,0:T(8,128)(2,1)} %grade.1.chunks), calls=%async_computation | async-start | bytes 786432 | tf_op jit(solution)/shard_map/all_to_all | solution.py:431
  11.9 0.7 %copy-start.1 = (f32[3]{0:T(128)S(1)}, f32[3]{0:T(128)}, u32[]{:S(2)}) copy-start(f32[3]{0:T(128)} %screen.1) | copy-start | bytes 40
  22.3 8.5 %collective-permute-start = (f32[3,3,16,8,128]{4,3,2,1,0:T(8,128)S(1)}, f32[3,3,16,8,128]{4,3,2,1,0:T(8,128)S(1)}, u32[]{:S(2)}, u32[]{:S(2)}) collective-permute-start(f32[3,3,16,8,128]{4,3,2,1,0:T(8,128)S(1)} %get-tuple-element.12), channel_id=1, source_target_pairs={{0,1},{1,0},{2,3},{3,2},{4,5},{5,4},{6,7},{7,6},{8,9},{9,8},{10,11... | collective-permute-start | bytes 1769480 | tf_op jit(solution)/shard_map/ppermute | solution.py:449

commit v8 on v7

--- a/solution.py
+++ b/solution.py
@@ -52,7 +52,7 @@
 
 def grade_kernel(
     w_in_at, b_in_at, w_out_at, b_out_at, screen_at, video_at, chunks,
-    w_in, b_in, w_out, b_out, screen, video, arrived, sent, graded, first, second, ready,
+    w_in, b_in, w_out, b_out, screen, video, arrived, sent, graded, first, ready,
 ):
     channels, rows, columns = video.shape[1:]
     units = b_in.shape[0]
@@ -95,7 +95,6 @@
         first[8 * j : 8 * j + 8] = three_parts(values, lane)
         for c in range(channels):
             out = jnp.full(TILE, w_out[c, j])
-            second[c, j] = out
             for k in range(channels + 1):
                 mix[c][k] = mix[c][k] + (0.5 * out) * into[k]
     for c in range(channels):
@@ -151,7 +150,7 @@
                     h = half[8 * j : 8 * j + 8]
                     unit = h * jnp.tanh(h)
                     for c in range(channels):
-                        total[c] = total[c] + wide(second[c, j]) * unit
+                        total[c] = total[c] + w_out[c, j] * unit
                 for c in range(channels):
                     for k in range(half_blocks):
                         tile = total[c][:, k * LANES : (k + 1) * LANES]
@@ -412,7 +411,6 @@
             pltpu.SemaphoreType.DMA((channels,)),
             pltpu.VMEM((channels, 2, rows // 2) + TILE, jnp.float32),
             pltpu.VMEM((8 * units, LANES), jnp.float32),
-            pltpu.VMEM((channels, units) + TILE, jnp.float32),
             pltpu.VMEM((channels, count) + chunk[1:], jnp.bfloat16),
         ],
         name="grade",

time: 32.3 us -> 32.2 us (level)
  no operation moved by 1% of the time
where the time goes in v8:
time: 32.2 us; the launch traced here: 32 us
  starting transfers between devices  8.59 us (27%)
  blocking collectives  7.89 us (25%)
  waiting for transfers between devices  7.77 us (24%)
  Pallas kernels  6.88 us (21%)
  local copies, waits for them, and re-layouts  0.71 us (2%)
    all_to_all x1, starting transfers between devices, shards(): held = lax.all_to_all(chunks, AXIS, 0, 0, axis_index_groups=[order])  8.01 us
    all_to_all x1, blocking collectives, shards(): sums = lax.all_to_all(sums, AXIS, 0, 0, axis_index_groups=[down])  7.89 us
    all_to_all x1, waiting for transfers between devices, shards(): held = lax.all_to_all(chunks, AXIS, 0, 0, axis_index_groups=[order])  7.76 us
    pallas_call x1, Pallas kernels, shards(): pl.pallas_call(grade_kernel, out_shape=jax.ShapeDtypeStruct((count,) + ch...  3.89 us
    pallas_call x1, Pallas kernels, shards(): pl.pallas_call(functools.partial(combine_kernel, columns), out_shape=jax....  1.17 us
    pallas_call x1, Pallas kernels, shards(): pl.pallas_call(functools.partial(moment_kernel, columns), out_shape=(jax....  1.15 us
    pallas_call x1, Pallas kernels, shards(): pl.pallas_call(fifth_kernel, out_shape=jax.ShapeDtypeStruct((channels + 1...  0.66 us
  transfers between devices with their start and end apart: 2, of which 1 were waited for; matrix products, arithmetic and copies ran while one was open for 0% of the time, Pallas kernels for 2%

profile of v8, /device:TPU:0, one launch (start us, length us, event | category | flops | bytes accessed | tf_op | source)
XLA Modules:
  0.0 32.0 jit_solution(11951816492321201105)
XLA Ops:
  0.0 3.9 %grade.1.chunks = bf16[16,3,2,16,128]{4,3,2,1,0:T(8,128)(2,1)} custom-call(f32[3,32]{1,0:T(4,128)} %bitcast.4, f32[32]{0:T(128)} %b_in_at.1, f32[3,32]{1,0:T(4,128)} %w_out_at.1, f32[3]{0:T(128)} %b_out_at.1, f32[3]{0:T(128)} %screen.1, bf16[1,3,32,960]{3,2,1,0:T(8,128)(2,1)} %video_at.1), custom_call_target="tpu_custom_call" | custom-call | tf_op jit(solution)/shard_map/grade/pallas_call | solution.py:402
  3.9 0.0 copy-start
  3.9 8.0 %all-to-all-start = ((bf16[16,3,2,16,128]{4,3,2,1,0:T(8,128)(2,1)}), bf16[16,3,2,16,128]{4,3,2,1,0:T(8,128)(2,1)S(1)}, u32[]{:S(2)}, u32[]{:S(2)}) async-start(bf16[16,3,2,16,128]{4,3,2,1,0:T(8,128)(2,1)} %grade.1.chunks), calls=%async_computation | async-start | bytes 786432 | tf_op jit(solution)/shard_map/all_to_all | solution.py:429
  11.9 0.0 copy-start.1
  11.9 0.0 copy-done
  11.9 0.6 %copy-done.1 = f32[3]{0:T(128)S(1)} copy-done((f32[3]{0:T(128)S(1)}, f32[3]{0:T(128)}, u32[]{:S(2)}) %copy-start.1) | copy-done | bytes 36
  12.6 0.7 %fifth.1.extra = f32[4,8,128]{2,1,0:T(8,128)S(1)} custom-call(f32[3]{0:T(128)S(1)} %copy-done.1, bf16[16,3,2,16,128]{4,3,2,1,0:T(8,128)(2,1)S(1)} %copy-done), custom_call_target="tpu_custom_call" | custom-call | flops 1048576 | bytes 1048576 | tf_op jit(solution)/shard_map/fifth/pallas_call | solution.py:418
  13.2 0.1 pad_maximum_fusion
  13.3 7.8 %all-to-all-done.held = bf16[16,3,2,16,128]{4,3,2,1,0:T(8,128)(2,1)S(1)} async-done(((bf16[16,3,2,16,128]{4,3,2,1,0:T(8,128)(2,1)}), bf16[16,3,2,16,128]{4,3,2,1,0:T(8,128)(2,1)S(1)}, u32[]{:S(2)}, u32[]{:S(2)}) %all-to-all-start) | async-done | bytes 393248 | tf_op jit(solution)/shard_map/all_to_all | solution.py:429
  21.1 0.1 broadcast_in_dim.2.place
  21.2 1.2 %moments.1 = (f32[16,1,128]{2,1,0:T(1,128)S(1)}, f32[3,3,16,8,128]{4,3,2,1,0:T(8,128)S(1)}, f32[3,3,16,8,128]{4,3,2,1,0:T(8,128)S(1)}, f32[8,128]{1,0:T(8,128)S(1)}) custom-call(f32[3,8,128]{2,1,0:T(8,128)S(1)} %broadcast_in_dim.2.place, bf16[16,3,2,16,128]{4,3,2,1,0:T(8,128)(2,1)S(1)} %all-to-all-done.held, f32[4,8,128]{2,1,0:T(8,128)S(1)} %fifth.1.extra), custom_call_target="tpu_custom_call" | custom-call | tf_op jit(solution)/shard_map/moments/pallas_call | solution.py:434
  22.3 0.6 %collective-permute-start = (f32[3,3,16,8,128]{4,3,2,1,0:T(8,128)S(1)}, f32[3,3,16,8,128]{4,3,2,1,0:T(8,128)S(1)}, u32[]{:S(2)}, u32[]{:S(2)}) collective-permute-start(f32[3,3,16,8,128]{4,3,2,1,0:T(8,128)S(1)} %get-tuple-element.12), channel_id=1, source_target_pairs={{0,1},{1,0},{2,3},{3,2},{4,5},{5,4},{6,7},{7,6},{8,9},{9,8},{10,11... | collective-permute-start | bytes 1769480 | tf_op jit(solution)/shard_map/ppermute | solution.py:447
  22.9 7.9 %all_to_all.10.sums = f32[16,1,128]{2,1,0:T(1,128)S(1)} all-to-all(f32[16,1,128]{2,1,0:T(1,128)S(1)} %get-tuple-element.10), channel_id=1, replica_groups={{15,14,13,12,11,10,9,8,7,6,5,4,3,2,1,0},{31,30,29,28,27,26,25,24,23,22,..., dimensions={0} | all-to-all | bytes 16384 | tf_op jit(solution)/shard_map/all_to_all | solution.py:449
  30.8 0.0 collective-permute-done.taken
  30.8 1.2 %combine.1 = f32[16,3,2,960]{3,2,1,0:T(2,128)} custom-call(f32[3,8,128]{2,1,0:T(8,128)S(1)} %broadcast_in_dim.2.place, f32[8,128]{1,0:T(8,128)S(1)} %get-tuple-element.9.sigma_at, f32[16,1,128]{2,1,0:T(1,128)S(1)} %all_to_all.10.sums, f32[3,3,16,8,128]{4,3,2,1,0:T(8,128)S(1)} %get-tuple-element.11.kept, f32[3,3,16,8,128]{4,3,2,1,0:T(8,128)S(1)} %collective-permute-done.taken), custom_call_target="tpu_custom_call" | custom-call | tf_op jit(solution)/shard_map/combine/pallas_call | solution.py:450
Async XLA Ops:
  3.9 8.0 %copy-start = (bf16[16,3,2,16,128]{4,3,2,1,0:T(8,128)(2,1)S(1)}, bf16[16,3,2,16,128]{4,3,2,1,0:T(8,128)(2,1)}, u32[]{:S(2)}) copy-start(bf16[16,3,2,16,128]{4,3,2,1,0:T(8,128)(2,1)} %grade.1.chunks) | copy-start | bytes 1179652
  3.9 17.2 %all-to-all-start = ((bf16[16,3,2,16,128]{4,3,2,1,0:T(8,128)(2,1)}), bf16[16,3,2,16,128]{4,3,2,1,0:T(8,128)(2,1)S(1)}, u32[]{:S(2)}, u32[]{:S(2)}) async-start(bf16[16,3,2,16,128]{4,3,2,1,0:T(8,128)(2,1)} %grade.1.chunks), calls=%async_computation | async-start | bytes 786432 | tf_op jit(solution)/shard_map/all_to_all | solution.py:429
  11.9 0.7 %copy-start.1 = (f32[3]{0:T(128)S(1)}, f32[3]{0:T(128)}, u32[]{:S(2)}) copy-start(f32[3]{0:T(128)} %screen.1) | copy-start | bytes 40
  22.3 8.5 %collective-permute-start = (f32[3,3,16,8,128]{4,3,2,1,0:T(8,128)S(1)}, f32[3,3,16,8,128]{4,3,2,1,0:T(8,128)S(1)}, u32[]{:S(2)}, u32[]{:S(2)}) collective-permute-start(f32[3,3,16,8,128]{4,3,2,1,0:T(8,128)S(1)} %get-tuple-element.12), channel_id=1, source_target_pairs={{0,1},{1,0},{2,3},{3,2},{4,5},{5,4},{6,7},{7,6},{8,9},{9,8},{10,11... | collective-permute-start | bytes 1769480 | tf_op jit(solution)/shard_map/ppermute | solution.py:447
